TPU v7x, 128 devices: a whole 4x4x4 slice. The times are simulated.
128 devices in a mesh: row: 16 (over y, z), col: 8 (over x, core).
Axes of the slice: x: 4, y: 4, z: 4, core: 2. Of those that a mesh axis runs over, the one named last changes fastest.
Arguments:
- panel_t: float32 [64, 16384], P(None, ('row', 'col')), may hold values from -0.1875 to 0.1875
- panel_grad_t: float32 [64, 16384], P(None, ('row', 'col')), may hold values from -1.2 to 1.2
- diag_factor: float32 [64, 64], replicated, may hold values from -0.1 to 2, as said below
- diag_grad: float32 [64, 64], replicated, may hold values from -3 to 3, as said below
- row_panel: float32 [64, 16384], P('row', 'col'), may hold values from -3 to 3
- row_grad: float32 [64, 16384], P('row', 'col'), may hold values from -3 to 3
- trailing: float32 [16384, 16384], P('row', 'col'), may hold values from -0.1875 to 0.1875
- trailing_grad: float32 [16384, 16384], P('row', 'col'), may hold values from -6 to 6
Outputs:
- panel_out: float32 [64, 16384], P(None, ('row', 'col'))
- trailing_out: float32 [16384, 16384], P('row', 'col')
- row_out: float32 [64, 16384], P('row', 'col')
- diag_out: float32 [64, 64], replicated
Inputs may be any that keep to these rules, and one draw needn't show every extreme that they name: `diag_factor`: lower triangular; diagonal between 1 and 2, entries below it within 0.1 in magnitude. `diag_grad`: lower triangular.
All inputs are finite; a program needn't handle non-finite values.
Results may differ from a plain program's by a relative error of at most 0.000078.
Values sent between devices are 32-bit elements; how exact they have to be, the bound alone decides.
No kernel may reach another device: no remote copies, remote signals or barrier semaphores. Data moves between devices by JAX's collectives and lax.ppermute only.
A program may use at most 64 MiB of HBM per device.

v0:
```python
import jax
import jax.numpy as jnp
from jax import lax
from jax.sharding import PartitionSpec as P


def solve_transposed(factor, values):
    return lax.linalg.triangular_solve(factor, values, left_side=True, lower=True, transpose_a=True)


def per_device(
    panel_t, panel_grad_t, diag_factor, diag_grad, row_panel, row_grad, trailing, trailing_grad
):
    highest = lax.Precision.HIGHEST
    full_row = lax.all_gather(row_panel, "row", axis=0, tiled=True)
    whole_t, whole_grad = (
        lax.all_gather(panel_t, "col", axis=1, tiled=True),
        lax.all_gather(panel_grad_t, "col", axis=1, tiled=True),
    )
    solved = solve_transposed(diag_factor, whole_grad)
    local_count = panel_t.shape[1]
    panel_out = lax.dynamic_slice_in_dim(
        solved, lax.axis_index("col") * local_count, local_count, 1
    )
    diag_term = jnp.dot(solved, whole_t.T, precision=highest)
    diag_sum = lax.psum(diag_term, "row")
    trailing_out = trailing_grad - jnp.dot(solved.T, full_row, precision=highest)
    partial_value = jnp.dot(solved, trailing, precision=highest)
    dsum = diag_grad - jnp.tril(diag_sum)
    phi = jnp.tril(jnp.dot(diag_factor.T, dsum, precision=highest))
    phi = phi - 0.5 * jnp.diag(jnp.diag(phi))
    inner = solve_transposed(diag_factor, phi)
    spart = lax.linalg.triangular_solve(
        diag_factor, inner, left_side=False, lower=True, transpose_a=False
    )
    both = spart + spart.T
    diag_out = 0.5 * both
    reduced = lax.psum_scatter(partial_value, "row", scatter_dimension=0, tiled=True)
    own_count = row_panel.shape[0]
    own_both = lax.dynamic_slice_in_dim(both, lax.axis_index("row") * own_count, own_count, 0)
    row_out = row_grad - reduced - jnp.dot(own_both, full_row, precision=highest)
    return (panel_out, trailing_out, row_out, diag_out)


def solution(mesh):
    return jax.shard_map(
        per_device,
        mesh=mesh,
        in_specs=(
            P(None, ("row", "col")),
            P(None, ("row", "col")),
            P(),
            P(),
            P("row", "col"),
            P("row", "col"),
            P("row", "col"),
            P("row", "col"),
        ),
        out_specs=(P(None, ("row", "col")), P("row", "col"), P("row", "col"), P()),
        check_vma=False,
    )
```

profile of v0, /device:TPU:0, one launch (start us, length us, event | category | flops | bytes accessed | tf_op | source)
XLA Modules:
  0.0 169.4 jit_solution(4801979914842837499)
XLA Ops:
  7.2 0.0 copy-start.5
  7.2 0.0 copy-start
  7.2 0.0 copy-start.1
  7.2 0.0 copy-start.4
  7.2 0.0 copy-start.2
  7.2 0.0 all-reduce.3.cloned.1.call-start
  7.3 0.8 select_bitcast_fusion
  8.0 4.9 %custom-call.7 = f32[1,64,64]{1,2,0:T(8,128)S(1)} custom-call(f32[1,64,64]{2,1,0:T(8,128)S(1)} %select_bitcast_fusion), custom_call_target="InvertDiagBlocksLowerTriangular" | custom-call | tf_op jit(solution)/shard_map/triangular_solve | solution.py:8
  12.9 13.5 %all_gather.9 = f32[64,1024]{1,0:T(8,128)S(1)} all-gather(f32[64,128]{1,0:T(8,128)} %param.9), channel_id=1, replica_groups=mesh['row'=16,'col'=8] {'col'}, dimensions={1}, use_global_device_ids=true | all-gather | bytes 294912 | tf_op jit(solution)/shard_map/all_gather | solution.py:18
  26.4 0.4 fusion.5
  26.8 8.3 %fusion.21 = f32[64,2048]{1,0:T(8,128)} fusion(f32[64,1024]{1,0:T(8,128)S(1)} %fusion.5, f32[1024,2048]{1,0:T(8,128)} %param.14), kind=kOutput, calls=%fused_computation.33 | convolution fusion | flops 1610612736 | bytes 9175040 | tf_op jit(solution)/shard_map/dot_general | solution.py:28
  35.0 0.0 all-reduce.3.cloned.1.call-update
  35.1 0.0 copy-done.1
  35.1 12.8 %all_gather.11 = f32[64,1024]{1,0:T(8,128)S(1)} all-gather(f32[64,128]{1,0:T(8,128)S(1)} %copy-done.1), channel_id=1, replica_groups=mesh['row'=16,'col'=8] {'col'}, dimensions={1}, use_global_device_ids=true | all-gather | bytes 294912 | tf_op jit(solution)/shard_map/all_gather | solution.py:17
  48.0 0.4 fusion.22
  48.3 75.9 %psum.7 = f32[64,64]{1,0:T(8,128)S(1)} all-reduce(f32[64,64]{1,0:T(8,128)S(1)} %fusion.22), channel_id=1, replica_groups=mesh['row'=16,'col'=8] {'row'}, use_global_device_ids=true, to_apply=%region_1.2 | all-reduce | flops 4096 | bytes 32768 | tf_op jit(solution)/shard_map/psum | solution.py:26
  124.3 0.0 copy-done
  124.3 0.0 copy-done.4
  124.3 0.2 fusion
  124.5 0.8 gather_fusion
  125.3 0.2 fusion.3
  125.6 0.2 fusion.1
  125.8 0.6 constant_dynamic-slice_fusion
  126.4 0.1 copy.17
  126.5 0.6 broadcast_multiply_fusion
  127.1 0.0 copy-done.2
  127.1 21.0 %all-gather = f32[16,4,2048]{2,1,0:T(4,128)S(1)} all-gather(f32[1,4,2048]{2,1,0:T(4,128)S(1)} %bitcast.30), channel_id=1, replica_groups=mesh['row'=16,'col'=8] {'row'}, dimensions={0}, use_global_device_ids=true | all-gather | bytes 557056 | tf_op jit(solution)/shard_map/all_gather | solution.py:15
  148.1 0.2 reshape.23
  148.3 0.0 copy-done.5
  148.3 0.6 dynamic-slice
  149.5 0.0 copy-start.3
  149.5 11.2 %convolution_subtract_fusion = f32[1024,2048]{1,0:T(8,128)} fusion(f32[1024,2048]{1,0:T(8,128)} %param.15, f32[64,1024]{1,0:T(8,128)S(1)} %fusion.5, f32[64,2048]{1,0:T(8,128)S(1)} %reshape.23), kind=kOutput, calls=%fused_computation.1 | convolution fusion | flops 1612709888 | bytes 17563648 | tf_op jit(solution)/shard_map/dot_general | solution.py:27
  160.7 0.0 all-reduce.3.cloned.1.call-done
  160.7 0.0 copy-done.3
  160.7 1.8 %convolution_subtract_fusion.1 = f32[4,2048]{1,0:T(4,128)} fusion(f32[64,2048]{1,0:T(8,128)S(1)} %reshape.23, f32[4,2048]{1,0:T(4,128)S(1)} %copy-done.3, f32[64,2048]{1,0:T(8,128)} %all-reduce.3.cloned.1.call-done, u32[]{:T(128)S(6)} %multiply.1, f32[64,64]{1,0:T(8,128)S(1)} %get-tuple-element.5, s32[]{:T(128)S(6)} %select_n.28), kind=kOutput, calls=%fused_computation.2 | convolution fusion | flops 6307840 | bytes 624648 | tf_op jit(solution)/shard_map/dot_general | solution.py:41
  (1 shorter events, 0.0 us)
Async XLA Ops:
  7.2 141.1 %copy-start.5 = (u32[128]{0:T(128)S(1)}, u32[128]{0:T(128)}, u32[]{:S(2)}) copy-start(u32[128]{0:T(128)} %constant.63) | copy-start | bytes 1540
  7.2 117.1 %copy-start = (f32[64,64]{1,0:T(8,128)S(1)}, f32[64,64]{1,0:T(8,128)}, u32[]{:S(2)}) copy-start(f32[64,64]{1,0:T(8,128)} %param.10) | copy-start | bytes 49156
  7.2 27.9 %copy-start.1 = (f32[64,128]{1,0:T(8,128)S(1)}, f32[64,128]{1,0:T(8,128)}, u32[]{:S(2)}) copy-start(f32[64,128]{1,0:T(8,128)} %param.8) | copy-start | bytes 98308
  7.2 117.1 %copy-start.4 = (f32[64,64]{1,0:T(8,128)S(1)}, f32[64,64]{1,0:T(8,128)}, u32[]{:S(2)}) copy-start(f32[64,64]{1,0:T(8,128)} %param.11) | copy-start | bytes 49156
  7.2 119.9 %copy-start.2 = (f32[4,2048]{1,0:T(4,128)S(1)}, f32[4,2048]{1,0:T(4,128)}, u32[]{:S(2)}) copy-start(f32[4,2048]{1,0:T(4,128)} %param.12) | copy-start | bytes 98308
  7.2 153.5 %all-reduce.3.cloned.1.call-start = ((), (), s32[]{:S(2)}) async-start(), calls=%async_computation | async-start | bytes 1048576
  149.5 11.2 %copy-start.3 = (f32[4,2048]{1,0:T(4,128)S(1)}, f32[4,2048]{1,0:T(4,128)}, u32[]{:S(2)}) copy-start(f32[4,2048]{1,0:T(4,128)} %param.13) | copy-start | bytes 98308
Sparse Core Ops, SparseCore 0:
  35.2 87.2 all-reduce.2
where the time goes:
time: 170 us; the launch traced here: 169 us
  blocking collectives  123 us (72%)
  matrix products  22.6 us (13%)
  between operations  14.8 us (9%)
  other arithmetic  6.3 us (4%)
  local copies, waits for them, and re-layouts  2.3 us (1%)
    psum x1, blocking collectives, per_device(): diag_sum = lax.psum(diag_term, 'row')  75.9 us
    all_gather x1, blocking collectives, per_device(): full_row = lax.all_gather(row_panel, 'row', axis=0, tiled=True)  21 us
    all_gather x1, blocking collectives, per_device(): lax.all_gather(panel_grad_t, 'col', axis=1, tiled=True)  13.5 us
    all_gather x1, blocking collectives, per_device(): lax.all_gather(panel_t, 'col', axis=1, tiled=True)  12.8 us
    dot_general x1, matrix products, per_device(): jnp.dot(solved.T, full_row, precision=highest)  11.2 us
    dot_general x1, matrix products, per_device(): partial_value = jnp.dot(solved, trailing, precision=highest)  8.27 us
    another operation x2, other arithmetic, solve_transposed(): lax.linalg.triangular_solve(factor, values, left_side=True, lower=True, t...  5.66 us
  transfers between devices with their start and end apart: 1, of which 0 were waited for; matrix products, arithmetic and copies ran while one was open for 9% of the time, Pallas kernels for 0%

commit v1 on v0

v1 whole, which is shorter than its diff:
```python
import jax
import jax.numpy as jnp
from jax import lax
from jax.experimental import pallas as pl
from jax.experimental.pallas import tpu as pltpu
from jax.sharding import PartitionSpec as P

N = 64
ROWS = 16
COLS = 8
LOCAL = 128
TILE_ROWS = COLS * LOCAL
TILE_COLS = 2048
OWN = N // ROWS
PIECES = TILE_COLS // 128
HIGHEST = lax.Precision.HIGHEST
F32 = jnp.float32
BF16 = jnp.bfloat16
MIB = 1024 * 1024


def dot(a, b, contract, precision=None):
    return lax.dot_general(
        a, b, ((contract[:1], contract[1:]), ((), ())), precision=precision, preferred_element_type=F32
    )


def split(value):
    high = value.astype(BF16)
    return high, (value - high.astype(F32)).astype(BF16)


def payload_kernel(grad_ref, panel_ref, out_ref):
    grad = grad_ref[...]
    term = dot(grad, panel_ref[...], (1, 1), HIGHEST)
    out_ref[:N, :] = grad
    out_ref[N:, :N] = term[: N // 2]
    out_ref[N:, N:] = term[N // 2 :]


def inverse_kernel(factor_ref, out_ref):
    factor = factor_ref[...]
    row = lax.broadcasted_iota(jnp.int32, (N, N), 0)
    col = lax.broadcasted_iota(jnp.int32, (N, N), 1)
    eye = jnp.where(row == col, 1.0, 0.0).astype(F32)
    diagonal = jnp.sum(factor * eye, axis=1, keepdims=True)
    diagonal_row = jnp.sum(factor * eye, axis=0, keepdims=True)
    below = jnp.where(row > col, factor, 0.0) / diagonal
    value = eye
    for j in range(N - 1):
        value = value - below[:, j : j + 1] * value[j : j + 1, :]
    out_ref[...] = value / diagonal_row


def product_kernel(
    near_ref, far_ref, inverse_ref, row_panel_ref, trailing_ref,
    own_ref, left_ref, send_ref,
    tile, gathered, rows, sems,
):
    chunk = 256
    copies = []
    for i in range(TILE_COLS // chunk):
        cols = pl.ds(i * chunk, chunk)
        copies.append(pltpu.make_async_copy(trailing_ref.at[:, cols], tile.at[:, cols], sems.at[i]))
        copies[-1].start()
    place = lax.axis_index("col")
    chip, core = place // 2, lax.rem(place, 2)
    for k in range(4):
        from_chip = lax.rem(chip - k + 4, 4) * 2
        for ref, which in ((near_ref, core), (far_ref, 1 - core)):
            start = pl.multiple_of((from_chip + which) * LOCAL, LOCAL)
            gathered[:, pl.ds(start, LOCAL)] = ref[k, :N, :]
    term = near_ref[0, N:, :] + far_ref[0, N:, :]
    for k in range(1, 4):
        term = term + near_ref[k, N:, :] + far_ref[k, N:, :]
    for j in range(PIECES):
        rows[OWN * j : OWN * (j + 1), :] = row_panel_ref[:, 128 * j : 128 * (j + 1)]
    own_rows = rows[...]
    for s in range(ROWS):
        send_ref[s, N : 2 * N, :] = own_rows
        send_ref[s, 2 * N :, :] = term
    solved = dot(inverse_ref[...], gathered[...], (0, 0), HIGHEST)
    gathered[...] = solved
    own_ref[...] = gathered[:, pl.ds(pl.multiple_of(place * LOCAL, LOCAL), LOCAL)]
    high, low = split(solved)
    both = jnp.concatenate([high, low], axis=0)
    doubled = jnp.concatenate([solved, solved], axis=0).T
    lane = lax.broadcasted_iota(jnp.int32, doubled.shape, 1)
    rounded = doubled.astype(BF16).astype(F32)
    pieces = jnp.where(lane < N, rounded, doubled - rounded).astype(BF16)
    left_ref[:, : 2 * N] = pieces
    left_ref[:, 2 * N :] = pieces
    for i in range(TILE_COLS // chunk):
        copies[i].wait()
        t_high, t_low = split(tile[:, i * chunk : (i + 1) * chunk])
        part = dot(both, t_high, (1, 0)) + dot(both, t_low, (1, 0))
        part = part[:N] + part[N:]
        for s in range(ROWS):
            for jj in range(chunk // 128):
                j = i * (chunk // 128) + jj
                send_ref[s, OWN * j : OWN * (j + 1), :] = part[OWN * s : OWN * (s + 1), 128 * jj : 128 * (jj + 1)]


def update_kernel(
    recv_ref, left_ref, inverse_ref, factor_ref, diag_grad_ref, row_grad_ref, grad_ref,
    out_ref, row_out_ref, diag_out_ref,
    grad, result, full, right, small, in_sems, out_sems,
):
    count = 8
    height = TILE_ROWS // count
    loads, stores = [], []
    for i in range(count):
        part = pl.ds(i * height, height)
        loads.append(pltpu.make_async_copy(grad_ref.at[part], grad.at[part], in_sems.at[i]))
        stores.append(pltpu.make_async_copy(result.at[part], out_ref.at[part], out_sems.at[i]))
        loads[-1].start()
    for s in range(ROWS):
        for j in range(PIECES):
            full[OWN * s : OWN * (s + 1), 128 * j : 128 * (j + 1)] = recv_ref[s, N + OWN * j : N + OWN * (j + 1), :]
    high, low = split(full[...])
    right[:N] = high
    right[N : 2 * N] = high
    right[2 * N : 3 * N] = low
    right[3 * N :] = low

    def step(i):
        loads[i].wait()
        part = slice(i * height, (i + 1) * height)
        result[part] = grad[part] - dot(left_ref[part], right[...], (1, 0))
        stores[i].start()

    for i in range(count // 2):
        step(i)

    packed = recv_ref[0, 2 * N :, :]
    reduced = recv_ref[0, :N, :]
    for s in range(1, ROWS):
        packed = packed + recv_ref[s, 2 * N :, :]
        reduced = reduced + recv_ref[s, :N, :]
    total = jnp.concatenate([packed[:, :N], packed[:, N:]], axis=0)
    inverse, factor = inverse_ref[...], factor_ref[...]
    r_id = lax.broadcasted_iota(jnp.int32, (N, N), 0)
    c_id = lax.broadcasted_iota(jnp.int32, (N, N), 1)
    lower = r_id >= c_id
    dsum = diag_grad_ref[...] - jnp.where(lower, dot(inverse, total, (0, 0), HIGHEST), 0.0)
    phi = jnp.where(lower, dot(factor, dsum, (0, 0), HIGHEST), 0.0)
    phi = jnp.where(r_id == c_id, 0.5 * phi, phi)
    spart = dot(dot(inverse, phi, (0, 0), HIGHEST), inverse, (1, 0), HIGHEST)
    both = spart + spart.T
    diag_out_ref[...] = 0.5 * both
    small[...] = both
    own_both = small[pl.ds(lax.axis_index("row") * OWN, OWN), :]
    both_high, both_low = split(own_both)
    wide = jnp.concatenate([both_high, both_low, both_high, both_low], axis=1)
    second = dot(wide, right[...], (1, 0))
    for j in range(PIECES):
        cols = slice(128 * j, 128 * (j + 1))
        row_out_ref[:, cols] = row_grad_ref[:, cols] - reduced[OWN * j : OWN * (j + 1), :] - second[:, cols]

    for i in range(count // 2, count):
        step(i)
    for copy in stores:
        copy.wait()


def across_chips(value, k):
    pairs = [(2 * x + c, 2 * ((x + k) % 4) + c) for x in range(4) for c in range(2)]
    return lax.ppermute(value, "col", pairs)


def per_device(panel_t, panel_grad_t, diag_factor, diag_grad, row_panel, row_grad, trailing, trailing_grad):
    vmem = pl.BlockSpec(memory_space=pltpu.VMEM)
    anywhere = pl.BlockSpec(memory_space=pl.ANY)
    payload = pl.pallas_call(
        payload_kernel,
        out_shape=jax.ShapeDtypeStruct((N + N // 2, LOCAL), F32),
        in_specs=[vmem, vmem],
        out_specs=vmem,
        name="payload",
    )(panel_grad_t, panel_t)
    opposite = across_chips(payload, 2)
    right = across_chips(payload, 1)
    left = across_chips(payload, 3)
    inverse = pl.pallas_call(
        inverse_kernel,
        out_shape=jax.ShapeDtypeStruct((N, N), F32),
        in_specs=[vmem],
        out_specs=vmem,
        name="inverse",
    )(diag_factor)
    near = jnp.stack([payload, right, opposite, left])
    far = lax.ppermute(near, "col", [(i, i ^ 1) for i in range(COLS)])
    panel_out, left_factor, send = pl.pallas_call(
        product_kernel,
        out_shape=(
            jax.ShapeDtypeStruct((N, LOCAL), F32),
            jax.ShapeDtypeStruct((TILE_ROWS, 4 * N), BF16),
            jax.ShapeDtypeStruct((ROWS, 2 * N + N // 2, 128), F32),
        ),
        in_specs=[vmem] * 4 + [anywhere],
        out_specs=(vmem,) * 3,
        scratch_shapes=[
            pltpu.VMEM((TILE_ROWS, TILE_COLS), F32),
            pltpu.VMEM((N, TILE_ROWS), F32),
            pltpu.VMEM((N, 128), F32),
            pltpu.SemaphoreType.DMA((8,)),
        ],
        compiler_params=pltpu.CompilerParams(vmem_limit_bytes=24 * MIB),
        name="product",
    )(near, far, inverse, row_panel, trailing)
    recv = lax.all_to_all(send, "row", 0, 0)
    trailing_out, row_out, diag_out = pl.pallas_call(
        update_kernel,
        out_shape=(
            jax.ShapeDtypeStruct((TILE_ROWS, TILE_COLS), F32),
            jax.ShapeDtypeStruct((OWN, TILE_COLS), F32),
            jax.ShapeDtypeStruct((N, N), F32),
        ),
        in_specs=[vmem] * 6 + [anywhere],
        out_specs=(anywhere, vmem, vmem),
        scratch_shapes=[
            pltpu.VMEM((TILE_ROWS, TILE_COLS), F32),
            pltpu.VMEM((TILE_ROWS, TILE_COLS), F32),
            pltpu.VMEM((N, TILE_COLS), F32),
            pltpu.VMEM((4 * N, TILE_COLS), BF16),
            pltpu.VMEM((N, N), F32),
            pltpu.SemaphoreType.DMA((8,)),
            pltpu.SemaphoreType.DMA((8,)),
        ],
        compiler_params=pltpu.CompilerParams(vmem_limit_bytes=32 * MIB),
        name="update",
    )(recv, left_factor, inverse, diag_factor, diag_grad, row_grad, trailing_grad)
    return (panel_out, trailing_out, row_out, diag_out)


def solution(mesh):
    return jax.shard_map(
        per_device,
        mesh=mesh,
        in_specs=(
            P(None, ("row", "col")),
            P(None, ("row", "col")),
            P(),
            P(),
            P("row", "col"),
            P("row", "col"),
            P("row", "col"),
            P("row", "col"),
        ),
        out_specs=(P(None, ("row", "col")), P("row", "col"), P("row", "col"), P()),
        check_vma=False,
    )
```

time: 170 us -> 61.1 us (0.36)
  blocking collectives: 123 us -> 28.2 us
  matrix products: 22.6 us -> 0 us
  Pallas kernels: 0 us -> 16.2 us
  between operations: 14.8 us -> 0.7 us
  other arithmetic: 6.3 us -> 0.82 us
  waiting for transfers between devices: 0.02 us -> 4.65 us
  starting transfers between devices: 0.04 us -> 4.61 us
  local copies, waits for them, and re-layouts: 2.3 us -> 5.56 us
    psum x1 -> x0, blocking collectives: 75.9 us -> none  [per_device(): diag_sum = lax.psum(diag_term, 'row')]
    all_gather x3 -> x0, blocking collectives: 47.3 us -> none  [the longest x1 21 us: per_device(): full_row = lax.all_gather(row_panel, 'row', axis=0, tiled=True)]
    all_to_all x0 -> x1, blocking collectives: none -> 28.2 us  [per_device(): recv = lax.all_to_all(send, 'row', 0, 0)]
    dot_general x5 -> x0, matrix products: 21.9 us -> none  [the longest x1 11.2 us: per_device(): jnp.dot(solved.T, full_row, precision=highest)]
    pallas_call x0 -> x4, Pallas kernels: none -> 16.2 us  [the longest x1 6.31 us: per_device(): pl.pallas_call(product_kernel, out_shape=(jax.ShapeDtypeStruct((N, LOCAL)...]
    another operation x2 -> x1, other arithmetic: 5.66 us -> 0.82 us  [per_device(): near = jnp.stack([payload, right, opposite, left])]
    unnamed x14 -> x16, local copies, waits for them, and re-layouts: 0.8 us -> 5.56 us
    ppermute x0 -> x4, waiting for transfers between devices: none -> 4.65 us  [the longest x3 4.64 us: across_chips(): return lax.ppermute(value, 'col', pairs)]
  transfers between devices with their start and end apart: 1 -> 4, of which waited for: 0 -> 3; matrix products, arithmetic and copies ran while one was open for 9% -> 0% of each run, Pallas kernels for 0% -> 4%
where the time goes in v1:
time: 61.1 us; the launch traced here: 60.7 us
  blocking collectives  28.2 us (46%)
  Pallas kernels  16.2 us (27%)
  local copies, waits for them, and re-layouts  5.56 us (9%)
  waiting for transfers between devices  4.65 us (8%)
  starting transfers between devices  4.61 us (8%)
  other arithmetic  0.82 us (1%)
  between operations  0.7 us (1%)
    all_to_all x1, blocking collectives, per_device(): recv = lax.all_to_all(send, 'row', 0, 0)  28.2 us
    pallas_call x1, Pallas kernels, per_device(): pl.pallas_call(product_kernel, out_shape=(jax.ShapeDtypeStruct((N, LOCAL)...  6.31 us
    pallas_call x1, Pallas kernels, per_device(): pl.pallas_call(update_kernel, out_shape=(jax.ShapeDtypeStruct((TILE_ROWS,...  5.98 us
    unnamed x16, local copies, waits for them, and re-layouts  5.56 us
    ppermute x3, waiting for transfers between devices, across_chips(): return lax.ppermute(value, 'col', pairs)  4.64 us
    ppermute x3, starting transfers between devices, across_chips(): return lax.ppermute(value, 'col', pairs)  4.53 us
    pallas_call x1, Pallas kernels, per_device(): pl.pallas_call(inverse_kernel, out_shape=jax.ShapeDtypeStruct((N, N), F32...  2.21 us
    pallas_call x1, Pallas kernels, per_device(): pl.pallas_call(payload_kernel, out_shape=jax.ShapeDtypeStruct((N + N // 2...  1.66 us
  transfers between devices with their start and end apart: 4, of which 3 were waited for; matrix products, arithmetic and copies ran while one was open for 0% of the time, Pallas kernels for 4%

profile of v1, /device:TPU:0, one launch (start us, length us, event | category | flops | bytes accessed | tf_op | source)
XLA Modules:
  0.0 60.7 jit_solution(3899410757479110530)
XLA Ops:
  0.6 0.0 copy-start.4
  0.6 0.0 copy-start.7
  0.7 0.0 copy-start.6
  0.7 1.7 %payload.1 = f32[96,128]{1,0:T(8,128)} custom-call(f32[64,128]{1,0:T(8,128)} %grad_ref.2, f32[64,128]{1,0:T(8,128)} %panel_ref.1), custom_call_target="tpu_custom_call" | custom-call | tf_op jit(solution)/shard_map/payload/pallas_call | solution.py:174
  2.3 2.8 %collective-permute-start.2 = (f32[96,128]{1,0:T(8,128)}, f32[96,128]{1,0:T(8,128)S(1)}, u32[]{:S(2)}, u32[]{:S(2)}) collective-permute-start(f32[96,128]{1,0:T(8,128)} %payload.1), channel_id=1, source_target_pairs={{0,6},{1,7},{2,0},{3,1},{4,2},{5,3},{6,4},{7,5},{8,14},{9,15},{10,... | collective-permute-start | bytes 147464 | tf_op jit(solution)/shard_map/ppermute | solution.py:168
  5.2 0.8 %collective-permute-start.1 = (f32[96,128]{1,0:T(8,128)}, f32[96,128]{1,0:T(8,128)S(1)}, u32[]{:S(2)}, u32[]{:S(2)}) collective-permute-start(f32[96,128]{1,0:T(8,128)} %payload.1), channel_id=1, source_target_pairs={{0,4},{1,5},{2,6},{3,7},{4,0},{5,1},{6,2},{7,3},{8,12},{9,13},{10,... | collective-permute-start | bytes 147464 | tf_op jit(solution)/shard_map/ppermute | solution.py:168
  6.0 0.9 %collective-permute-start = (f32[96,128]{1,0:T(8,128)}, f32[96,128]{1,0:T(8,128)S(1)}, u32[]{:S(2)}, u32[]{:S(2)}) collective-permute-start(f32[96,128]{1,0:T(8,128)} %payload.1), channel_id=1, source_target_pairs={{0,2},{1,3},{2,4},{3,5},{4,6},{5,7},{6,0},{7,1},{8,10},{9,11},{10,... | collective-permute-start | bytes 147464 | tf_op jit(solution)/shard_map/ppermute | solution.py:168
  6.9 0.5 collective-permute-done.2
  7.4 3.6 %collective-permute-done.1 = f32[96,128]{1,0:T(8,128)S(1)} collective-permute-done((f32[96,128]{1,0:T(8,128)}, f32[96,128]{1,0:T(8,128)S(1)}, u32[]{:S(2)}, u32[]{:S(2)}) %collective-permute-start.1) | collective-permute-done | bytes 49184 | tf_op jit(solution)/shard_map/ppermute | solution.py:168
  11.0 0.5 collective-permute-done
  11.5 0.8 %pad_maximum_fusion.near_ref = f32[4,96,128]{2,1,0:T(8,128)S(1)} fusion(f32[1,96,128]{2,1,0:T(8,128)S(1)} %bitcast.5, f32[1,96,128]{2,1,0:T(8,128)S(1)} %bitcast.6, f32[1,96,128]{2,1,0:T(8,128)S(1)} %bitcast.7, f32[1,96,128]{2,1,0:T(8,128)} %bitcast.4), kind=kLoop, calls=%fused_computation | loop fusion | flops 147456 | bytes 393216 | tf_op jit(solution)/shard_map/stack | solution.py:191
  12.3 0.1 collective-permute-start.3
  12.4 2.2 %inverse.1.inverse_ref = f32[64,64]{1,0:T(8,128)} custom-call(f32[64,64]{1,0:T(8,128)} %factor_ref.3), custom_call_target="tpu_custom_call" | custom-call | tf_op jit(solution)/shard_map/inverse/pallas_call | solution.py:184
  14.6 0.0 copy-start
  14.6 0.0 collective-permute-done.3.far_ref
  14.6 0.0 copy-start.1
  14.6 3.5 %copy-done.1 = f32[1024,2048]{1,0:T(8,128)S(1)} copy-done((f32[1024,2048]{1,0:T(8,128)S(1)}, f32[1024,2048]{1,0:T(8,128)}, u32[]{:S(2)}) %copy-start.1) | copy-done | bytes 8388632
  18.2 0.0 copy-start.2
  18.2 1.0 %copy-done.2 = f32[64,64]{1,0:T(8,128)S(1)} copy-done((f32[64,64]{1,0:T(8,128)S(1)}, f32[64,64]{1,0:T(8,128)}, u32[]{:S(2)}) %copy-start.2) | copy-done | bytes 16408
  19.2 0.0 copy-start.5
  19.2 1.0 %copy-done.5 = f32[4,2048]{1,0:T(4,128)S(1)} copy-done((f32[4,2048]{1,0:T(4,128)S(1)}, f32[4,2048]{1,0:T(4,128)}, u32[]{:S(2)}) %copy-start.5) | copy-done | bytes 32792
  20.2 0.0 copy-start.3
  20.2 6.3 %product.1 = (f32[64,128]{1,0:T(8,128)}, bf16[1024,256]{1,0:T(8,128)(2,1)S(1)}, f32[16,160,128]{2,1,0:T(8,128)S(1)}) custom-call(f32[4,96,128]{2,1,0:T(8,128)S(1)} %pad_maximum_fusion.near_ref, f32[4,96,128]{2,1,0:T(8,128)S(1)} %collective-permute-done.3.far_ref, f32[64,64]{1,0:T(8,128)S(1)} %copy-done.2, f32[4,2048]{1,0:T(4,128)S(1)} %copy-done.5, ...), custom_call_target="tpu_custom_call" | custom-call | tf_op jit(solution)/shard_map/product/pallas_call | solution.py:193
  26.5 28.2 %all_to_all.5.recv_ref = f32[16,160,128]{2,1,0:T(8,128)S(1)} all-to-all(f32[16,160,128]{2,1,0:T(8,128)S(1)} %get-tuple-element.11), channel_id=1, replica_groups=mesh['row'=16,'col'=8] {'row'}, dimensions={0} | all-to-all | bytes 2621440 | tf_op jit(solution)/shard_map/all_to_all | solution.py:211
  54.7 0.0 copy-done.4
  54.7 0.0 copy-done.7
  54.7 0.0 copy-done.6
  54.7 0.0 copy-done
  54.7 0.0 copy-done.3
  54.8 6.0 %update.1 = (f32[1024,2048]{1,0:T(8,128)}, f32[4,2048]{1,0:T(4,128)}, f32[64,64]{1,0:T(8,128)}) custom-call(f32[16,160,128]{2,1,0:T(8,128)S(1)} %all_to_all.5.recv_ref, bf16[1024,256]{1,0:T(8,128)(2,1)S(1)} %get-tuple-element.12.left_ref, f32[64,64]{1,0:T(8,128)S(1)} %copy-done.3, f32[64,64]{1,0:T(8,128)S(1)} %copy-done.4, f32[64,64]{1,0:T(8,128)S(1)} %copy-done.6, ...), custom_call_target="tpu_custom_call" | custom-call | tf_op jit(solution)/shard_map/update/pallas_call | solution.py:212
Async XLA Ops:
  0.6 54.1 %copy-start.4 = (f32[64,64]{1,0:T(8,128)S(1)}, f32[64,64]{1,0:T(8,128)}, u32[]{:S(2)}) copy-start(f32[64,64]{1,0:T(8,128)} %factor_ref.3) | copy-start | bytes 49156
  0.6 54.1 %copy-start.7 = (f32[4,2048]{1,0:T(4,128)S(1)}, f32[4,2048]{1,0:T(4,128)}, u32[]{:S(2)}) copy-start(f32[4,2048]{1,0:T(4,128)} %row_grad_ref.1) | copy-start | bytes 98308
  0.7 54.1 %copy-start.6 = (f32[64,64]{1,0:T(8,128)S(1)}, f32[64,64]{1,0:T(8,128)}, u32[]{:S(2)}) copy-start(f32[64,64]{1,0:T(8,128)} %diag_grad_ref.1) | copy-start | bytes 49156
  2.3 5.0 %collective-permute-start.2 = (f32[96,128]{1,0:T(8,128)}, f32[96,128]{1,0:T(8,128)S(1)}, u32[]{:S(2)}, u32[]{:S(2)}) collective-permute-start(f32[96,128]{1,0:T(8,128)} %payload.1), channel_id=1, source_target_pairs={{0,6},{1,7},{2,0},{3,1},{4,2},{5,3},{6,4},{7,5},{8,14},{9,15},{10,... | collective-permute-start | bytes 147464 | tf_op jit(solution)/shard_map/ppermute | solution.py:168
  5.2 5.8 %collective-permute-start.1 = (f32[96,128]{1,0:T(8,128)}, f32[96,128]{1,0:T(8,128)S(1)}, u32[]{:S(2)}, u32[]{:S(2)}) collective-permute-start(f32[96,128]{1,0:T(8,128)} %payload.1), channel_id=1, source_target_pairs={{0,4},{1,5},{2,6},{3,7},{4,0},{5,1},{6,2},{7,3},{8,12},{9,13},{10,... | collective-permute-start | bytes 147464 | tf_op jit(solution)/shard_map/ppermute | solution.py:168
  6.0 5.5 %collective-permute-start = (f32[96,128]{1,0:T(8,128)}, f32[96,128]{1,0:T(8,128)S(1)}, u32[]{:S(2)}, u32[]{:S(2)}) collective-permute-start(f32[96,128]{1,0:T(8,128)} %payload.1), channel_id=1, source_target_pairs={{0,2},{1,3},{2,4},{3,5},{4,6},{5,7},{6,0},{7,1},{8,10},{9,11},{10,... | collective-permute-start | bytes 147464 | tf_op jit(solution)/shard_map/ppermute | solution.py:168
  12.3 2.3 %collective-permute-start.3 = (f32[4,96,128]{2,1,0:T(8,128)S(1)}, f32[4,96,128]{2,1,0:T(8,128)S(1)}, u32[]{:S(2)}, u32[]{:S(2)}) collective-permute-start(f32[4,96,128]{2,1,0:T(8,128)S(1)} %pad_maximum_fusion.near_ref), channel_id=1, source_target_pairs={{0,1},{1,0},{2,3},{3,2},{4,5},{5,4},{6,7},{7,6},{8,9},{9,8},{10,11... | collective-permute-start | bytes 589832 | tf_op jit(solution)/shard_map/ppermute | solution.py:192
  14.6 40.1 %copy-start = (f32[1024,2048]{1,0:T(8,128)S(1)}, f32[1024,2048]{1,0:T(8,128)}, u32[]{:S(2)}) copy-start(f32[1024,2048]{1,0:T(8,128)} %grad_ref.3) | copy-start | bytes 25165828
  14.6 3.5 %copy-start.1 = (f32[1024,2048]{1,0:T(8,128)S(1)}, f32[1024,2048]{1,0:T(8,128)}, u32[]{:S(2)}) copy-start(f32[1024,2048]{1,0:T(8,128)} %trailing_ref.1) | copy-start | bytes 25165828
  18.2 1.0 %copy-start.2 = (f32[64,64]{1,0:T(8,128)S(1)}, f32[64,64]{1,0:T(8,128)}, u32[]{:S(2)}) copy-start(f32[64,64]{1,0:T(8,128)} %inverse.1.inverse_ref) | copy-start | bytes 49156
  19.2 1.0 %copy-start.5 = (f32[4,2048]{1,0:T(4,128)S(1)}, f32[4,2048]{1,0:T(4,128)}, u32[]{:S(2)}) copy-start(f32[4,2048]{1,0:T(4,128)} %row_panel_ref.1) | copy-start | bytes 98308
  20.2 34.6 %copy-start.3 = (f32[64,64]{1,0:T(8,128)S(1)}, f32[64,64]{1,0:T(8,128)}, u32[]{:S(2)}) copy-start(f32[64,64]{1,0:T(8,128)} %inverse.1.inverse_ref) | copy-start | bytes 49156

commit v2 on v1

--- a/solution.py
+++ b/solution.py
@@ -38,7 +38,8 @@
     out_ref[N:, N:] = term[N // 2 :]
 
 
-def inverse_kernel(factor_ref, out_ref):
+def inverse_kernel(factor_ref, payload_ref, out_ref, copy_ref):
+    copy_ref[...] = payload_ref[...]
     factor = factor_ref[...]
     row = lax.broadcasted_iota(jnp.int32, (N, N), 0)
     col = lax.broadcasted_iota(jnp.int32, (N, N), 1)
@@ -55,14 +56,9 @@
 def product_kernel(
     near_ref, far_ref, inverse_ref, row_panel_ref, trailing_ref,
     own_ref, left_ref, send_ref,
-    tile, gathered, rows, sems,
+    gathered, rows,
 ):
     chunk = 256
-    copies = []
-    for i in range(TILE_COLS // chunk):
-        cols = pl.ds(i * chunk, chunk)
-        copies.append(pltpu.make_async_copy(trailing_ref.at[:, cols], tile.at[:, cols], sems.at[i]))
-        copies[-1].start()
     place = lax.axis_index("col")
     chip, core = place // 2, lax.rem(place, 2)
     for k in range(4):
@@ -91,8 +87,7 @@
     left_ref[:, : 2 * N] = pieces
     left_ref[:, 2 * N :] = pieces
     for i in range(TILE_COLS // chunk):
-        copies[i].wait()
-        t_high, t_low = split(tile[:, i * chunk : (i + 1) * chunk])
+        t_high, t_low = split(trailing_ref[:, i * chunk : (i + 1) * chunk])
         part = dot(both, t_high, (1, 0)) + dot(both, t_low, (1, 0))
         part = part[:N] + part[N:]
         for s in range(ROWS):
@@ -104,16 +99,14 @@
 def update_kernel(
     recv_ref, left_ref, inverse_ref, factor_ref, diag_grad_ref, row_grad_ref, grad_ref,
     out_ref, row_out_ref, diag_out_ref,
-    grad, result, full, right, small, in_sems, out_sems,
+    result, full, right, small, out_sems,
 ):
     count = 8
     height = TILE_ROWS // count
-    loads, stores = [], []
+    stores = []
     for i in range(count):
         part = pl.ds(i * height, height)
-        loads.append(pltpu.make_async_copy(grad_ref.at[part], grad.at[part], in_sems.at[i]))
         stores.append(pltpu.make_async_copy(result.at[part], out_ref.at[part], out_sems.at[i]))
-        loads[-1].start()
     for s in range(ROWS):
         for j in range(PIECES):
             full[OWN * s : OWN * (s + 1), 128 * j : 128 * (j + 1)] = recv_ref[s, N + OWN * j : N + OWN * (j + 1), :]
@@ -124,9 +117,8 @@
     right[3 * N :] = low
 
     def step(i):
-        loads[i].wait()
         part = slice(i * height, (i + 1) * height)
-        result[part] = grad[part] - dot(left_ref[part], right[...], (1, 0))
+        result[part] = grad_ref[part] - dot(left_ref[part], right[...], (1, 0))
         stores[i].start()
 
     for i in range(count // 2):
@@ -176,18 +168,20 @@
         out_shape=jax.ShapeDtypeStruct((N + N // 2, LOCAL), F32),
         in_specs=[vmem, vmem],
         out_specs=vmem,
+        compiler_params=pltpu.CompilerParams(vmem_limit_bytes=MIB),
         name="payload",
     )(panel_grad_t, panel_t)
     opposite = across_chips(payload, 2)
     right = across_chips(payload, 1)
     left = across_chips(payload, 3)
-    inverse = pl.pallas_call(
+    inverse, payload = pl.pallas_call(
         inverse_kernel,
-        out_shape=jax.ShapeDtypeStruct((N, N), F32),
-        in_specs=[vmem],
-        out_specs=vmem,
+        out_shape=(jax.ShapeDtypeStruct((N, N), F32), jax.ShapeDtypeStruct((N + N // 2, LOCAL), F32)),
+        in_specs=[vmem, vmem],
+        out_specs=(vmem, vmem),
+        compiler_params=pltpu.CompilerParams(vmem_limit_bytes=MIB),
         name="inverse",
-    )(diag_factor)
+    )(diag_factor, payload)
     near = jnp.stack([payload, right, opposite, left])
     far = lax.ppermute(near, "col", [(i, i ^ 1) for i in range(COLS)])
     panel_out, left_factor, send = pl.pallas_call(
@@ -197,13 +191,11 @@
             jax.ShapeDtypeStruct((TILE_ROWS, 4 * N), BF16),
             jax.ShapeDtypeStruct((ROWS, 2 * N + N // 2, 128), F32),
         ),
-        in_specs=[vmem] * 4 + [anywhere],
+        in_specs=[vmem] * 5,
         out_specs=(vmem,) * 3,
         scratch_shapes=[
-            pltpu.VMEM((TILE_ROWS, TILE_COLS), F32),
             pltpu.VMEM((N, TILE_ROWS), F32),
             pltpu.VMEM((N, 128), F32),
-            pltpu.SemaphoreType.DMA((8,)),
         ],
         compiler_params=pltpu.CompilerParams(vmem_limit_bytes=24 * MIB),
         name="product",
@@ -216,15 +208,13 @@
             jax.ShapeDtypeStruct((OWN, TILE_COLS), F32),
             jax.ShapeDtypeStruct((N, N), F32),
         ),
-        in_specs=[vmem] * 6 + [anywhere],
+        in_specs=[vmem] * 7,
         out_specs=(anywhere, vmem, vmem),
         scratch_shapes=[
-            pltpu.VMEM((TILE_ROWS, TILE_COLS), F32),
             pltpu.VMEM((TILE_ROWS, TILE_COLS), F32),
             pltpu.VMEM((N, TILE_COLS), F32),
             pltpu.VMEM((4 * N, TILE_COLS), BF16),
             pltpu.VMEM((N, N), F32),
-            pltpu.SemaphoreType.DMA((8,)),
             pltpu.SemaphoreType.DMA((8,)),
         ],
         compiler_params=pltpu.CompilerParams(vmem_limit_bytes=32 * MIB),

time: 61.1 us -> 52.1 us (0.85)
  Pallas kernels: 16.2 us -> 7.53 us
  local copies, waits for them, and re-layouts: 5.56 us -> 6.73 us
  other arithmetic: 0.82 us -> 0.01 us
    pallas_call x1, Pallas kernels: 6.31 us -> 1.93 us  [per_device(): pl.pallas_call(product_kernel, out_shape=(jax.ShapeDtypeStruct((N, LOCAL)...]
    ppermute x3, waiting for transfers between devices: 4.64 us -> 2.82 us  [across_chips(): return lax.ppermute(value, 'col', pairs)]
    pallas_call x1, Pallas kernels: 5.98 us -> 4.53 us  [per_device(): pl.pallas_call(update_kernel, out_shape=(jax.ShapeDtypeStruct((TILE_ROWS,...]
    pallas_call x1, Pallas kernels: 1.66 us -> 0.23 us  [per_device(): pl.pallas_call(payload_kernel, out_shape=jax.ShapeDtypeStruct((N + N // 2...]
    ppermute x1, waiting for transfers between devices: 0.01 us -> 1.43 us  [per_device(): far = lax.ppermute(near, 'col', [(i, i ^ 1) for i in range(COLS)])]
    pallas_call x1, Pallas kernels: 2.21 us -> 0.84 us  [per_device(): pl.pallas_call(inverse_kernel, out_shape=(jax.ShapeDtypeStruct((N, N), F3...]
    unnamed x16 -> x18, local copies, waits for them, and re-layouts: 5.56 us -> 6.73 us
    another operation x1, other arithmetic: 0.82 us -> 0.01 us  [per_device(): near = jnp.stack([payload, right, opposite, left])]
  transfers between devices with their start and end apart: 4 -> 4, of which waited for: 3 -> 3; matrix products, arithmetic and copies ran while one was open for 0% -> 0% of each run, Pallas kernels for 4% -> 2%
where the time goes in v2:
time: 52.1 us; the launch traced here: 51.8 us
  blocking collectives  27.9 us (54%)
  Pallas kernels  7.53 us (14%)
  local copies, waits for them, and re-layouts  6.73 us (13%)
  starting transfers between devices  4.64 us (9%)
  waiting for transfers between devices  4.25 us (8%)
  between operations  0.7 us (1%)
    all_to_all x1, blocking collectives, per_device(): recv = lax.all_to_all(send, 'row', 0, 0)  27.9 us
    unnamed x18, local copies, waits for them, and re-layouts  6.73 us
    ppermute x3, starting transfers between devices, across_chips(): return lax.ppermute(value, 'col', pairs)  4.55 us
    pallas_call x1, Pallas kernels, per_device(): pl.pallas_call(update_kernel, out_shape=(jax.ShapeDtypeStruct((TILE_ROWS,...  4.53 us
    ppermute x3, waiting for transfers between devices, across_chips(): return lax.ppermute(value, 'col', pairs)  2.82 us
    pallas_call x1, Pallas kernels, per_device(): pl.pallas_call(product_kernel, out_shape=(jax.ShapeDtypeStruct((N, LOCAL)...  1.93 us
    ppermute x1, waiting for transfers between devices, per_device(): far = lax.ppermute(near, 'col', [(i, i ^ 1) for i in range(COLS)])  1.43 us
  transfers between devices with their start and end apart: 4, of which 3 were waited for; matrix products, arithmetic and copies ran while one was open for 0% of the time, Pallas kernels for 2%

profile of v2, /device:TPU:0, one launch (start us, length us, event | category | flops | bytes accessed | tf_op | source)
XLA Modules:
  0.0 51.8 jit_solution(12054881191936536770)
XLA Ops:
  0.6 0.0 copy-start
  0.6 0.0 copy-start.7
  0.7 0.9 %copy-done.7 = f32[64,128]{1,0:T(8,128)S(1)} copy-done((f32[64,128]{1,0:T(8,128)S(1)}, f32[64,128]{1,0:T(8,128)}, u32[]{:S(2)}) %copy-start.7) | copy-done | bytes 32792
  1.6 0.0 copy-start.8
  1.6 0.9 %copy-done.8 = f32[64,128]{1,0:T(8,128)S(1)} copy-done((f32[64,128]{1,0:T(8,128)S(1)}, f32[64,128]{1,0:T(8,128)}, u32[]{:S(2)}) %copy-start.8) | copy-done | bytes 32792
  2.5 0.2 payload.1.payload_ref
  2.7 2.9 %collective-permute-start.2 = (f32[96,128]{1,0:T(8,128)S(1)}, f32[96,128]{1,0:T(8,128)S(1)}, u32[]{:S(2)}, u32[]{:S(2)}) collective-permute-start(f32[96,128]{1,0:T(8,128)S(1)} %payload.1.payload_ref), channel_id=1, source_target_pairs={{0,6},{1,7},{2,0},{3,1},{4,2},{5,3},{6,4},{7,5},{8,14},{9,15},{10,... | collective-permute-start | bytes 147464 | tf_op jit(solution)/shard_map/ppermute | solution.py:160
  5.6 0.8 %collective-permute-start.1 = (f32[96,128]{1,0:T(8,128)S(1)}, f32[96,128]{1,0:T(8,128)S(1)}, u32[]{:S(2)}, u32[]{:S(2)}) collective-permute-start(f32[96,128]{1,0:T(8,128)S(1)} %payload.1.payload_ref), channel_id=1, source_target_pairs={{0,4},{1,5},{2,6},{3,7},{4,0},{5,1},{6,2},{7,3},{8,12},{9,13},{10,... | collective-permute-start | bytes 147464 | tf_op jit(solution)/shard_map/ppermute | solution.py:160
  6.4 0.9 %collective-permute-start = (f32[96,128]{1,0:T(8,128)S(1)}, f32[96,128]{1,0:T(8,128)S(1)}, u32[]{:S(2)}, u32[]{:S(2)}) collective-permute-start(f32[96,128]{1,0:T(8,128)S(1)} %payload.1.payload_ref), channel_id=1, source_target_pairs={{0,2},{1,3},{2,4},{3,5},{4,6},{5,7},{6,0},{7,1},{8,10},{9,11},{10,... | collective-permute-start | bytes 147464 | tf_op jit(solution)/shard_map/ppermute | solution.py:160
  7.3 0.0 copy-start.2
  7.3 0.8 %copy-done.2 = f32[64,64]{1,0:T(8,128)S(1)} copy-done((f32[64,64]{1,0:T(8,128)S(1)}, f32[64,64]{1,0:T(8,128)}, u32[]{:S(2)}) %copy-start.2) | copy-done | bytes 16408
  8.0 0.8 %inverse.1 = (f32[64,64]{1,0:T(8,128)S(1)}, f32[96,128]{1,0:T(8,128)S(1)}) custom-call(f32[64,64]{1,0:T(8,128)S(1)} %copy-done.2, f32[96,128]{1,0:T(8,128)S(1)} %payload.1.payload_ref), custom_call_target="tpu_custom_call" | custom-call | tf_op jit(solution)/shard_map/inverse/pallas_call | solution.py:177
  8.9 0.0 collective-permute-done.2
  8.9 2.3 %collective-permute-done.1 = f32[96,128]{1,0:T(8,128)S(1)} collective-permute-done((f32[96,128]{1,0:T(8,128)S(1)}, f32[96,128]{1,0:T(8,128)S(1)}, u32[]{:S(2)}, u32[]{:S(2)}) %collective-permute-start.1) | collective-permute-done | bytes 49184 | tf_op jit(solution)/shard_map/ppermute | solution.py:160
  11.2 0.5 %collective-permute-done = f32[96,128]{1,0:T(8,128)S(1)} collective-permute-done((f32[96,128]{1,0:T(8,128)S(1)}, f32[96,128]{1,0:T(8,128)S(1)}, u32[]{:S(2)}, u32[]{:S(2)}) %collective-permute-start) | collective-permute-done | bytes 49184 | tf_op jit(solution)/shard_map/ppermute | solution.py:160
  11.7 0.1 collective-permute-start.3
  11.8 1.4 %collective-permute-done.3.far_ref = f32[4,96,128]{2,1,0:T(8,128)S(1)} collective-permute-done((f32[4,96,128]{2,1,0:T(8,128)S(1)}, f32[4,96,128]{2,1,0:T(8,128)S(1)}, u32[]{:S(2)}, u32[]{:S(2)}) %collective-permute-start.3) | collective-permute-done | bytes 196640 | tf_op jit(solution)/shard_map/ppermute | solution.py:186
  13.2 0.0 copy-start.1
  13.2 3.4 %copy-done.1 = f32[1024,2048]{1,0:T(8,128)S(1)} copy-done((f32[1024,2048]{1,0:T(8,128)S(1)}, f32[1024,2048]{1,0:T(8,128)}, u32[]{:S(2)}) %copy-start.1) | copy-done | bytes 8388632
  16.6 0.0 copy-start.4
  16.6 0.8 %copy-done.4 = f32[4,2048]{1,0:T(4,128)S(1)} copy-done((f32[4,2048]{1,0:T(4,128)S(1)}, f32[4,2048]{1,0:T(4,128)}, u32[]{:S(2)}) %copy-start.4) | copy-done | bytes 32792
  17.4 0.0 copy-start.3
  17.4 0.0 copy-start.5
  17.4 0.0 copy-start.6
  17.4 1.9 %product.1 = (f32[64,128]{1,0:T(8,128)}, bf16[1024,256]{1,0:T(8,128)(2,1)S(1)}, f32[16,160,128]{2,1,0:T(8,128)S(1)}) custom-call(f32[4,96,128]{2,1,0:T(8,128)S(1)} %pad_maximum_fusion.near_ref, f32[4,96,128]{2,1,0:T(8,128)S(1)} %collective-permute-done.3.far_ref, f32[64,64]{1,0:T(8,128)S(1)} %get-tuple-element.13.inverse_ref, f32[4,2048]{1,0:T(4,128)S(1)} %copy-done.4, ...), custom_call_target="tpu_custom_call" | custom-call | tf_op jit(solution)/shard_map/product/pallas_call | solution.py:187
  19.3 27.9 %all_to_all.5.recv_ref = f32[16,160,128]{2,1,0:T(8,128)S(1)} all-to-all(f32[16,160,128]{2,1,0:T(8,128)S(1)} %get-tuple-element.15), channel_id=1, replica_groups=mesh['row'=16,'col'=8] {'row'}, dimensions={0} | all-to-all | bytes 2621440 | tf_op jit(solution)/shard_map/all_to_all | solution.py:203
  47.2 0.0 copy-done
  47.2 0.0 copy-done.3
  47.2 0.0 copy-done.5
  47.2 0.0 copy-done.6
  47.2 4.5 %update.1 = (f32[1024,2048]{1,0:T(8,128)}, f32[4,2048]{1,0:T(4,128)}, f32[64,64]{1,0:T(8,128)}) custom-call(f32[16,160,128]{2,1,0:T(8,128)S(1)} %all_to_all.5.recv_ref, bf16[1024,256]{1,0:T(8,128)(2,1)S(1)} %get-tuple-element.16.left_ref, f32[64,64]{1,0:T(8,128)S(1)} %get-tuple-element.13.inverse_ref, f32[64,64]{1,0:T(8,128)S(1)} %copy-done.3, ...), custom_call_target="tpu_custom_call" | custom-call | tf_op jit(solution)/shard_map/update/pallas_call | solution.py:204
  (1 shorter events, 0.0 us)
Async XLA Ops:
  0.6 46.6 %copy-start = (f32[1024,2048]{1,0:T(8,128)S(1)}, f32[1024,2048]{1,0:T(8,128)}, u32[]{:S(2)}) copy-start(f32[1024,2048]{1,0:T(8,128)} %grad_ref.3) | copy-start | bytes 25165828
  0.6 0.9 %copy-start.7 = (f32[64,128]{1,0:T(8,128)S(1)}, f32[64,128]{1,0:T(8,128)}, u32[]{:S(2)}) copy-start(f32[64,128]{1,0:T(8,128)} %grad_ref.2) | copy-start | bytes 98308
  1.6 0.9 %copy-start.8 = (f32[64,128]{1,0:T(8,128)S(1)}, f32[64,128]{1,0:T(8,128)}, u32[]{:S(2)}) copy-start(f32[64,128]{1,0:T(8,128)} %panel_ref.1) | copy-start | bytes 98308
  2.7 6.2 %collective-permute-start.2 = (f32[96,128]{1,0:T(8,128)S(1)}, f32[96,128]{1,0:T(8,128)S(1)}, u32[]{:S(2)}, u32[]{:S(2)}) collective-permute-start(f32[96,128]{1,0:T(8,128)S(1)} %payload.1.payload_ref), channel_id=1, source_target_pairs={{0,6},{1,7},{2,0},{3,1},{4,2},{5,3},{6,4},{7,5},{8,14},{9,15},{10,... | collective-permute-start | bytes 147464 | tf_op jit(solution)/shard_map/ppermute | solution.py:160
  5.6 5.6 %collective-permute-start.1 = (f32[96,128]{1,0:T(8,128)S(1)}, f32[96,128]{1,0:T(8,128)S(1)}, u32[]{:S(2)}, u32[]{:S(2)}) collective-permute-start(f32[96,128]{1,0:T(8,128)S(1)} %payload.1.payload_ref), channel_id=1, source_target_pairs={{0,4},{1,5},{2,6},{3,7},{4,0},{5,1},{6,2},{7,3},{8,12},{9,13},{10,... | collective-permute-start | bytes 147464 | tf_op jit(solution)/shard_map/ppermute | solution.py:160
  6.4 5.3 %collective-permute-start = (f32[96,128]{1,0:T(8,128)S(1)}, f32[96,128]{1,0:T(8,128)S(1)}, u32[]{:S(2)}, u32[]{:S(2)}) collective-permute-start(f32[96,128]{1,0:T(8,128)S(1)} %payload.1.payload_ref), channel_id=1, source_target_pairs={{0,2},{1,3},{2,4},{3,5},{4,6},{5,7},{6,0},{7,1},{8,10},{9,11},{10,... | collective-permute-start | bytes 147464 | tf_op jit(solution)/shard_map/ppermute | solution.py:160
  7.3 0.8 %copy-start.2 = (f32[64,64]{1,0:T(8,128)S(1)}, f32[64,64]{1,0:T(8,128)}, u32[]{:S(2)}) copy-start(f32[64,64]{1,0:T(8,128)} %factor_ref.3) | copy-start | bytes 49156
  11.7 1.5 %collective-permute-start.3 = (f32[4,96,128]{2,1,0:T(8,128)S(1)}, f32[4,96,128]{2,1,0:T(8,128)S(1)}, u32[]{:S(2)}, u32[]{:S(2)}) collective-permute-start(f32[4,96,128]{2,1,0:T(8,128)S(1)} %pad_maximum_fusion.near_ref), channel_id=1, source_target_pairs={{0,1},{1,0},{2,3},{3,2},{4,5},{5,4},{6,7},{7,6},{8,9},{9,8},{10,11... | collective-permute-start | bytes 589832 | tf_op jit(solution)/shard_map/ppermute | solution.py:186
  13.2 3.4 %copy-start.1 = (f32[1024,2048]{1,0:T(8,128)S(1)}, f32[1024,2048]{1,0:T(8,128)}, u32[]{:S(2)}) copy-start(f32[1024,2048]{1,0:T(8,128)} %trailing_ref.1) | copy-start | bytes 25165828
  16.6 0.8 %copy-start.4 = (f32[4,2048]{1,0:T(4,128)S(1)}, f32[4,2048]{1,0:T(4,128)}, u32[]{:S(2)}) copy-start(f32[4,2048]{1,0:T(4,128)} %row_panel_ref.1) | copy-start | bytes 98308
  17.4 29.8 %copy-start.3 = (f32[64,64]{1,0:T(8,128)S(1)}, f32[64,64]{1,0:T(8,128)}, u32[]{:S(2)}) copy-start(f32[64,64]{1,0:T(8,128)} %factor_ref.3) | copy-start | bytes 49156
  17.4 29.8 %copy-start.5 = (f32[64,64]{1,0:T(8,128)S(1)}, f32[64,64]{1,0:T(8,128)}, u32[]{:S(2)}) copy-start(f32[64,64]{1,0:T(8,128)} %diag_grad_ref.1) | copy-start | bytes 49156
  17.4 29.8 %copy-start.6 = (f32[4,2048]{1,0:T(4,128)S(1)}, f32[4,2048]{1,0:T(4,128)}, u32[]{:S(2)}) copy-start(f32[4,2048]{1,0:T(4,128)} %row_grad_ref.1) | copy-start | bytes 98308

commit v3 on v2

v3 whole, which is shorter than its diff:
```python
import jax
import jax.numpy as jnp
from jax import lax
from jax.experimental import pallas as pl
from jax.experimental.pallas import tpu as pltpu
from jax.sharding import PartitionSpec as P

N = 64
ROWS = 16
COLS = 8
LOCAL = 128
TILE_ROWS = COLS * LOCAL
TILE_COLS = 2048
OWN = N // ROWS
PIECES = TILE_COLS // 128
HIGHEST = lax.Precision.HIGHEST
F32 = jnp.float32
BF16 = jnp.bfloat16
MIB = 1024 * 1024


def dot(a, b, contract, precision=None):
    return lax.dot_general(
        a, b, ((contract[:1], contract[1:]), ((), ())), precision=precision, preferred_element_type=F32
    )


def split(value):
    high = value.astype(BF16)
    return high, (value - high.astype(F32)).astype(BF16)


def block_row(k, other):
    place = lax.axis_index("col")
    chip, core = place // 2, lax.rem(place, 2)
    core = 1 - core if other else core
    return pl.multiple_of((lax.rem(chip - k + 4, 4) * 2 + core) * LOCAL, LOCAL)


def prepare_kernel(
    payload_ref, factor_ref, row_panel_ref,
    inverse_ref, copy_ref, rows_ref,
):
    copy_ref[...] = payload_ref[...]
    factor = factor_ref[...]
    row = lax.broadcasted_iota(jnp.int32, (N, N), 0)
    col = lax.broadcasted_iota(jnp.int32, (N, N), 1)
    eye = jnp.where(row == col, 1.0, 0.0).astype(F32)
    diagonal = jnp.sum(factor * eye, axis=1, keepdims=True)
    diagonal_row = jnp.sum(factor * eye, axis=0, keepdims=True)
    below = jnp.where(row > col, factor, 0.0) / diagonal
    value = eye
    for j in range(N - 1):
        value = value - below[:, j : j + 1] * value[j : j + 1, :]
    inverse_ref[...] = value / diagonal_row
    for j in range(PIECES):
        rows_ref[OWN * j : OWN * (j + 1), :] = row_panel_ref[:, 128 * j : 128 * (j + 1)]


def solve_line(line_ref, inverse_ref, left_ref):
    grads = jnp.concatenate([line_ref[k, :N, :] for k in range(4)], axis=1)
    panels = jnp.concatenate([line_ref[k, N:, :] for k in range(4)], axis=1)
    solved = dot(inverse_ref[...], grads, (0, 0), HIGHEST)
    high, low = split(solved)
    both = jnp.concatenate([high, low], axis=0)
    panel_high, panel_low = split(panels)
    term = dot(both, panel_high, (1, 1)) + dot(both, panel_low, (1, 1))
    doubled = jnp.concatenate([solved, solved], axis=0).T
    lane = lax.broadcasted_iota(jnp.int32, doubled.shape, 1)
    rounded = doubled.astype(BF16).astype(F32)
    pieces = jnp.where(lane < N, rounded, doubled - rounded).astype(BF16)
    left_ref[:, : 2 * N] = pieces
    left_ref[:, 2 * N :] = pieces
    return solved, both, term[:N] + term[N:]


def line_product(both, tile_ref, cols, other):
    tile = jnp.concatenate([tile_ref[pl.ds(block_row(k, other), LOCAL), cols] for k in range(4)], axis=0)
    t_high, t_low = split(tile)
    part = dot(both, t_high, (1, 0)) + dot(both, t_low, (1, 0))
    return part[:N] + part[N:]


CHUNK = 256


def near_kernel(
    near_ref, inverse_ref, tile_ref,
    own_ref, left_ref, term_ref, part_ref,
):
    solved, both, term = solve_line(near_ref, inverse_ref, left_ref)
    own_ref[...] = solved[:, :LOCAL]
    term_ref[...] = term
    for i in range(TILE_COLS // CHUNK):
        cols = slice(i * CHUNK, (i + 1) * CHUNK)
        part_ref[:, cols] = line_product(both, tile_ref, cols, False)


def far_kernel(
    far_ref, inverse_ref, rows_ref, tile_ref, near_term_ref, near_part_ref,
    left_ref, send_ref,
):
    own_rows = rows_ref[...]
    for s in range(ROWS):
        send_ref[s, N : 2 * N, :] = own_rows
    _, both, term = solve_line(far_ref, inverse_ref, left_ref)
    term = term + near_term_ref[...]
    packed = jnp.concatenate([term[: N // 2], term[N // 2 :]], axis=1)
    for s in range(ROWS):
        send_ref[s, 2 * N :, :] = packed
    for i in range(TILE_COLS // CHUNK):
        cols = slice(i * CHUNK, (i + 1) * CHUNK)
        part = near_part_ref[:, cols] + line_product(both, tile_ref, cols, True)
        for s in range(ROWS):
            for jj in range(CHUNK // 128):
                j = i * (CHUNK // 128) + jj
                send_ref[s, OWN * j : OWN * (j + 1), :] = part[OWN * s : OWN * (s + 1), 128 * jj : 128 * (jj + 1)]


def update_kernel(
    recv_ref, near_left_ref, far_left_ref, inverse_ref, factor_ref, diag_grad_ref, row_grad_ref, grad_ref,
    out_ref, row_out_ref, diag_out_ref,
    result, full, right, small, out_sems,
):
    for s in range(ROWS):
        for j in range(PIECES):
            full[OWN * s : OWN * (s + 1), 128 * j : 128 * (j + 1)] = recv_ref[s, N + OWN * j : N + OWN * (j + 1), :]
    high, low = split(full[...])
    right[:N] = high
    right[N : 2 * N] = high
    right[2 * N : 3 * N] = low
    right[3 * N :] = low
    stores = []

    def step(left_ref, k, other):
        part = pl.ds(block_row(k, other), LOCAL)
        result[part] = grad_ref[part] - dot(left_ref[k * LOCAL : (k + 1) * LOCAL], right[...], (1, 0))
        stores.append(pltpu.make_async_copy(result.at[part], out_ref.at[part], out_sems.at[len(stores)]))
        stores[-1].start()

    for k in range(4):
        step(near_left_ref, k, False)

    packed = recv_ref[0, 2 * N :, :]
    reduced = recv_ref[0, :N, :]
    for s in range(1, ROWS):
        packed = packed + recv_ref[s, 2 * N :, :]
        reduced = reduced + recv_ref[s, :N, :]
    total = jnp.concatenate([packed[:, :N], packed[:, N:]], axis=0)
    inverse, factor = inverse_ref[...], factor_ref[...]
    r_id = lax.broadcasted_iota(jnp.int32, (N, N), 0)
    c_id = lax.broadcasted_iota(jnp.int32, (N, N), 1)
    lower = r_id >= c_id
    dsum = diag_grad_ref[...] - jnp.where(lower, total, 0.0)
    phi = jnp.where(lower, dot(factor, dsum, (0, 0), HIGHEST), 0.0)
    phi = jnp.where(r_id == c_id, 0.5 * phi, phi)
    spart = dot(dot(inverse, phi, (0, 0), HIGHEST), inverse, (1, 0), HIGHEST)
    both = spart + spart.T
    diag_out_ref[...] = 0.5 * both
    small[...] = both
    own_both = small[pl.ds(lax.axis_index("row") * OWN, OWN), :]
    both_high, both_low = split(own_both)
    wide = jnp.concatenate([both_high, both_low, both_high, both_low], axis=1)
    second = dot(wide, right[...], (1, 0))
    for j in range(PIECES):
        cols = slice(128 * j, 128 * (j + 1))
        row_out_ref[:, cols] = row_grad_ref[:, cols] - reduced[OWN * j : OWN * (j + 1), :] - second[:, cols]

    for k in range(4):
        step(far_left_ref, k, True)
    for copy in stores:
        copy.wait()


def across_chips(value, k):
    pairs = [(2 * x + c, 2 * ((x + k) % 4) + c) for x in range(4) for c in range(2)]
    return lax.ppermute(value, "col", pairs)


def per_device(panel_t, panel_grad_t, diag_factor, diag_grad, row_panel, row_grad, trailing, trailing_grad):
    vmem = pl.BlockSpec(memory_space=pltpu.VMEM)
    anywhere = pl.BlockSpec(memory_space=pl.ANY)
    payload = jnp.pad(panel_grad_t, ((0, N), (0, 0))) + jnp.pad(panel_t, ((N, 0), (0, 0)))
    opposite = across_chips(payload, 2)
    right = across_chips(payload, 1)
    left = across_chips(payload, 3)
    inverse, payload, rows = pl.pallas_call(
        prepare_kernel,
        out_shape=(
            jax.ShapeDtypeStruct((N, N), F32),
            jax.ShapeDtypeStruct((2 * N, LOCAL), F32),
            jax.ShapeDtypeStruct((N, 128), F32),
        ),
        in_specs=[vmem] * 3,
        out_specs=(vmem,) * 3,
        compiler_params=pltpu.CompilerParams(vmem_limit_bytes=4 * MIB),
        cost_estimate=pl.CostEstimate(flops=4_000_000_000, bytes_accessed=0, transcendentals=0),
        name="prepare",
    )(payload, diag_factor, row_panel)
    near = jnp.stack([payload, right, opposite, left])
    far = lax.ppermute(near, "col", [(i, i ^ 1) for i in range(COLS)])
    panel_out, near_left, near_term, near_part = pl.pallas_call(
        near_kernel,
        out_shape=(
            jax.ShapeDtypeStruct((N, LOCAL), F32),
            jax.ShapeDtypeStruct((TILE_ROWS // 2, 4 * N), BF16),
            jax.ShapeDtypeStruct((N, N), F32),
            jax.ShapeDtypeStruct((N, TILE_COLS), F32),
        ),
        in_specs=[vmem] * 3,
        out_specs=(vmem,) * 4,
        compiler_params=pltpu.CompilerParams(vmem_limit_bytes=16 * MIB),
        cost_estimate=pl.CostEstimate(flops=1_000_000_000, bytes_accessed=0, transcendentals=0),
        name="near",
    )(near, inverse, trailing)
    far_left, send = pl.pallas_call(
        far_kernel,
        out_shape=(
            jax.ShapeDtypeStruct((TILE_ROWS // 2, 4 * N), BF16),
            jax.ShapeDtypeStruct((ROWS, 2 * N + N // 2, 128), F32),
        ),
        in_specs=[vmem] * 6,
        out_specs=(vmem,) * 2,
        compiler_params=pltpu.CompilerParams(vmem_limit_bytes=16 * MIB),
        name="far",
    )(far, inverse, rows, trailing, near_term, near_part)
    recv = lax.all_to_all(send, "row", 0, 0)
    trailing_out, row_out, diag_out = pl.pallas_call(
        update_kernel,
        out_shape=(
            jax.ShapeDtypeStruct((TILE_ROWS, TILE_COLS), F32),
            jax.ShapeDtypeStruct((OWN, TILE_COLS), F32),
            jax.ShapeDtypeStruct((N, N), F32),
        ),
        in_specs=[vmem] * 8,
        out_specs=(anywhere, vmem, vmem),
        scratch_shapes=[
            pltpu.VMEM((TILE_ROWS, TILE_COLS), F32),
            pltpu.VMEM((N, TILE_COLS), F32),
            pltpu.VMEM((4 * N, TILE_COLS), BF16),
            pltpu.VMEM((N, N), F32),
            pltpu.SemaphoreType.DMA((8,)),
        ],
        compiler_params=pltpu.CompilerParams(vmem_limit_bytes=32 * MIB),
        name="update",
    )(recv, near_left, far_left, inverse, diag_factor, diag_grad, row_grad, trailing_grad)
    return (panel_out, trailing_out, row_out, diag_out)


def solution(mesh):
    return jax.shard_map(
        per_device,
        mesh=mesh,
        in_specs=(
            P(None, ("row", "col")),
            P(None, ("row", "col")),
            P(),
            P(),
            P("row", "col"),
            P("row", "col"),
            P("row", "col"),
            P("row", "col"),
        ),
        out_specs=(P(None, ("row", "col")), P("row", "col"), P("row", "col"), P()),
        check_vma=False,
    )
```

time: 52.1 us -> 46.7 us (0.90)
  local copies, waits for them, and re-layouts: 6.73 us -> 1.56 us
  waiting for transfers between devices: 4.25 us -> 2.45 us
  other arithmetic: 0.01 us -> 0.95 us
    unnamed x18, local copies, waits for them, and re-layouts: 6.73 us -> 1.56 us
    ppermute x1, waiting for transfers between devices: 1.43 us -> 0.04 us  [per_device(): far = lax.ppermute(near, 'col', [(i, i ^ 1) for i in range(COLS)])]
    add x0 -> x1, other arithmetic: none -> 0.93 us  [per_device(): jnp.pad(panel_grad_t, ((0, N), (0, 0))) + jnp.pad(panel_t, ((N, 0), (0, 0)))]
  transfers between devices with their start and end apart: 4 -> 4, of which waited for: 3 -> 2; matrix products, arithmetic and copies ran while one was open for 0% -> 0% of each run, Pallas kernels for 2% -> 5%
where the time goes in v3:
time: 46.7 us; the launch traced here: 46.5 us
  blocking collectives  28.2 us (60%)
  Pallas kernels  7.89 us (17%)
  starting transfers between devices  4.67 us (10%)
  waiting for transfers between devices  2.45 us (5%)
  local copies, waits for them, and re-layouts  1.56 us (3%)
  other arithmetic  0.95 us (2%)
  between operations  0.76 us (2%)
    all_to_all x1, blocking collectives, per_device(): recv = lax.all_to_all(send, 'row', 0, 0)  28.2 us
    ppermute x3, starting transfers between devices, across_chips(): return lax.ppermute(value, 'col', pairs)  4.58 us
    pallas_call x1, Pallas kernels, per_device(): pl.pallas_call(update_kernel, out_shape=(jax.ShapeDtypeStruct((TILE_ROWS,...  4.39 us
    ppermute x3, waiting for transfers between devices, across_chips(): return lax.ppermute(value, 'col', pairs)  2.42 us
    unnamed x18, local copies, waits for them, and re-layouts  1.56 us
    pallas_call x1, Pallas kernels, per_device(): pl.pallas_call(near_kernel, out_shape=(jax.ShapeDtypeStruct((N, LOCAL), F...  1.41 us
    pallas_call x1, Pallas kernels, per_device(): pl.pallas_call(far_kernel, out_shape=(jax.ShapeDtypeStruct((TILE_ROWS //...  1.25 us
  transfers between devices with their start and end apart: 4, of which 2 were waited for; matrix products, arithmetic and copies ran while one was open for 0% of the time, Pallas kernels for 5%

profile of v3, /device:TPU:0, one launch (start us, length us, event | category | flops | bytes accessed | tf_op | source)
XLA Modules:
  0.0 46.5 jit_solution(1964082989249462973)
XLA Ops:
  0.6 0.0 slice-start
  0.6 0.9 %pad_add_fusion.payload_ref = f32[128,128]{1,0:T(8,128)S(1)} fusion(f32[64,128]{1,0:T(8,128)} %param.8, f32[64,128]{1,0:T(8,128)} %param.9), kind=kLoop, calls=%fused_computation.1 | loop fusion | flops 16384 | bytes 131072 | tf_op jit(solution)/shard_map/add | solution.py:183
  1.6 0.0 slice-start.1
  1.6 2.9 %collective-permute-start.2 = (f32[128,128]{1,0:T(8,128)S(1)}, f32[128,128]{1,0:T(8,128)S(1)}, u32[]{:S(2)}, u32[]{:S(2)}) collective-permute-start(f32[128,128]{1,0:T(8,128)S(1)} %pad_add_fusion.payload_ref), channel_id=1, source_target_pairs={{0,6},{1,7},{2,0},{3,1},{4,2},{5,3},{6,4},{7,5},{8,14},{9,15},{10,... | collective-permute-start | bytes 196616 | tf_op jit(solution)/shard_map/ppermute | solution.py:177
  4.5 0.8 %collective-permute-start.1 = (f32[128,128]{1,0:T(8,128)S(1)}, f32[128,128]{1,0:T(8,128)S(1)}, u32[]{:S(2)}, u32[]{:S(2)}) collective-permute-start(f32[128,128]{1,0:T(8,128)S(1)} %pad_add_fusion.payload_ref), channel_id=1, source_target_pairs={{0,4},{1,5},{2,6},{3,7},{4,0},{5,1},{6,2},{7,3},{8,12},{9,13},{10,... | collective-permute-start | bytes 196616 | tf_op jit(solution)/shard_map/ppermute | solution.py:177
  5.3 0.9 %collective-permute-start = (f32[128,128]{1,0:T(8,128)S(1)}, f32[128,128]{1,0:T(8,128)S(1)}, u32[]{:S(2)}, u32[]{:S(2)}) collective-permute-start(f32[128,128]{1,0:T(8,128)S(1)} %pad_add_fusion.payload_ref), channel_id=1, source_target_pairs={{0,2},{1,3},{2,4},{3,5},{4,6},{5,7},{6,0},{7,1},{8,10},{9,11},{10,... | collective-permute-start | bytes 196616 | tf_op jit(solution)/shard_map/ppermute | solution.py:177
  6.2 0.0 copy-start
  6.2 0.8 %copy-done = f32[64,64]{1,0:T(8,128)S(1)} copy-done((f32[64,64]{1,0:T(8,128)S(1)}, f32[64,64]{1,0:T(8,128)}, u32[]{:S(2)}) %copy-start) | copy-done | bytes 16408
  6.9 0.0 copy-start.4
  6.9 0.8 %copy-done.4 = f32[4,2048]{1,0:T(4,128)S(1)} copy-done((f32[4,2048]{1,0:T(4,128)S(1)}, f32[4,2048]{1,0:T(4,128)}, u32[]{:S(2)}) %copy-start.4) | copy-done | bytes 32792
  7.7 0.8 %prepare.1 = (f32[64,64]{1,0:T(8,128)S(1)}, f32[128,128]{1,0:T(8,128)S(1)}, f32[64,128]{1,0:T(8,128)S(1)}) custom-call(f32[128,128]{1,0:T(8,128)S(1)} %pad_add_fusion.payload_ref, f32[64,64]{1,0:T(8,128)S(1)} %copy-done, f32[4,2048]{1,0:T(4,128)S(1)} %copy-done.4), custom_call_target="tpu_custom_call" | custom-call | flops 4000000000 | tf_op jit(solution)/shard_map/prepare/pallas_call | solution.py:187
  8.5 0.0 collective-permute-done.2
  8.5 1.7 %collective-permute-done.1 = f32[128,128]{1,0:T(8,128)S(1)} collective-permute-done((f32[128,128]{1,0:T(8,128)S(1)}, f32[128,128]{1,0:T(8,128)S(1)}, u32[]{:S(2)}, u32[]{:S(2)}) %collective-permute-start.1) | collective-permute-done | bytes 65568 | tf_op jit(solution)/shard_map/ppermute | solution.py:177
  10.3 0.7 %collective-permute-done = f32[128,128]{1,0:T(8,128)S(1)} collective-permute-done((f32[128,128]{1,0:T(8,128)S(1)}, f32[128,128]{1,0:T(8,128)S(1)}, u32[]{:S(2)}, u32[]{:S(2)}) %collective-permute-start) | collective-permute-done | bytes 65568 | tf_op jit(solution)/shard_map/ppermute | solution.py:177
  11.0 0.1 collective-permute-start.3
  11.1 0.0 slice-done
  11.1 0.0 slice-done.1
  11.1 0.0 slice-start.2
  11.1 0.0 copy-start.1
  11.1 0.0 copy-start.2
  11.1 0.0 copy-start.3
  11.1 1.4 %near.1 = (f32[64,128]{1,0:T(8,128)}, bf16[512,256]{1,0:T(8,128)(2,1)S(1)}, f32[64,64]{1,0:T(8,128)S(1)}, f32[64,2048]{1,0:T(8,128)S(1)}) custom-call(f32[4,128,128]{2,1,0:T(8,128)S(1)} %pad_maximum_fusion.near_ref, f32[64,64]{1,0:T(8,128)S(1)} %get-tuple-element.17.inverse_ref, f32[1024,2048]{1,0:T(8,128)S(1)} %bitcast.5), custom_call_target="tpu_custom_call" | custom-call | flops 1000000000 | tf_op jit(solution)/shard_map/near/pallas_call | solution.py:202
  12.5 0.0 collective-permute-done.3.far_ref
  12.6 0.0 slice-start.3
  12.6 1.3 %far.1 = (bf16[512,256]{1,0:T(8,128)(2,1)S(1)}, f32[16,160,128]{2,1,0:T(8,128)S(1)}) custom-call(f32[4,128,128]{2,1,0:T(8,128)S(1)} %collective-permute-done.3.far_ref, f32[64,64]{1,0:T(8,128)S(1)} %get-tuple-element.17.inverse_ref, f32[64,128]{1,0:T(8,128)S(1)} %get-tuple-element.19.rows_ref, f32[1024,2048]{1,0:T(8,128)S(1)} %bitcast.5, ...), custom_call_target="tpu_custom_call" | custom-call | tf_op jit(solution)/shard_map/far/pallas_call | solution.py:216
  13.8 28.2 %all_to_all.5.recv_ref = f32[16,160,128]{2,1,0:T(8,128)S(1)} all-to-all(f32[16,160,128]{2,1,0:T(8,128)S(1)} %get-tuple-element.22), channel_id=1, replica_groups=mesh['row'=16,'col'=8] {'row'}, dimensions={0} | all-to-all | bytes 2621440 | tf_op jit(solution)/shard_map/all_to_all | solution.py:227
  42.0 0.0 slice-done.2
  42.0 0.0 copy-done.1
  42.1 0.0 copy-done.2
  42.1 0.0 copy-done.3
  42.1 0.0 slice-done.3
  42.1 4.4 %update.1 = (f32[1024,2048]{1,0:T(8,128)}, f32[4,2048]{1,0:T(4,128)}, f32[64,64]{1,0:T(8,128)}) custom-call(f32[16,160,128]{2,1,0:T(8,128)S(1)} %all_to_all.5.recv_ref, bf16[512,256]{1,0:T(8,128)(2,1)S(1)} %get-tuple-element.23.near_left_ref, bf16[512,256]{1,0:T(8,128)(2,1)S(1)} %get-tuple-element.24.far_left_ref, ...), custom_call_target="tpu_custom_call" | custom-call | tf_op jit(solution)/shard_map/update/pallas_call | solution.py:228
  (3 shorter events, 0.0 us)
Async XLA Ops:
  0.6 10.4 %slice-start = ((s8[8388608]{0:T(1024)(128)(4,1)}), s8[4194304]{0:T(1024)(128)(4,1)S(1)}, s32[]{:S(2)}) async-start(s8[8388608]{0:T(1024)(128)(4,1)} %bitcast.4), calls=%async_computation.1 | async-start | bytes 8388608
  1.6 9.5 %slice-start.1 = ((s8[8388608]{0:T(1024)(128)(4,1)}), s8[4194304]{0:T(1024)(128)(4,1)S(1)}, s32[]{:S(2)}) async-start(s8[8388608]{0:T(1024)(128)(4,1)} %bitcast.4), calls=%async_computation.2 | async-start | bytes 8388608
  1.6 6.9 %collective-permute-start.2 = (f32[128,128]{1,0:T(8,128)S(1)}, f32[128,128]{1,0:T(8,128)S(1)}, u32[]{:S(2)}, u32[]{:S(2)}) collective-permute-start(f32[128,128]{1,0:T(8,128)S(1)} %pad_add_fusion.payload_ref), channel_id=1, source_target_pairs={{0,6},{1,7},{2,0},{3,1},{4,2},{5,3},{6,4},{7,5},{8,14},{9,15},{10,... | collective-permute-start | bytes 196616 | tf_op jit(solution)/shard_map/ppermute | solution.py:177
  4.5 5.8 %collective-permute-start.1 = (f32[128,128]{1,0:T(8,128)S(1)}, f32[128,128]{1,0:T(8,128)S(1)}, u32[]{:S(2)}, u32[]{:S(2)}) collective-permute-start(f32[128,128]{1,0:T(8,128)S(1)} %pad_add_fusion.payload_ref), channel_id=1, source_target_pairs={{0,4},{1,5},{2,6},{3,7},{4,0},{5,1},{6,2},{7,3},{8,12},{9,13},{10,... | collective-permute-start | bytes 196616 | tf_op jit(solution)/shard_map/ppermute | solution.py:177
  5.3 5.7 %collective-permute-start = (f32[128,128]{1,0:T(8,128)S(1)}, f32[128,128]{1,0:T(8,128)S(1)}, u32[]{:S(2)}, u32[]{:S(2)}) collective-permute-start(f32[128,128]{1,0:T(8,128)S(1)} %pad_add_fusion.payload_ref), channel_id=1, source_target_pairs={{0,2},{1,3},{2,4},{3,5},{4,6},{5,7},{6,0},{7,1},{8,10},{9,11},{10,... | collective-permute-start | bytes 196616 | tf_op jit(solution)/shard_map/ppermute | solution.py:177
  6.2 0.8 %copy-start = (f32[64,64]{1,0:T(8,128)S(1)}, f32[64,64]{1,0:T(8,128)}, u32[]{:S(2)}) copy-start(f32[64,64]{1,0:T(8,128)} %factor_ref.3) | copy-start | bytes 49156
  6.9 0.8 %copy-start.4 = (f32[4,2048]{1,0:T(4,128)S(1)}, f32[4,2048]{1,0:T(4,128)}, u32[]{:S(2)}) copy-start(f32[4,2048]{1,0:T(4,128)} %row_panel_ref.1) | copy-start | bytes 98308
  11.0 1.6 %collective-permute-start.3 = (f32[4,128,128]{2,1,0:T(8,128)S(1)}, f32[4,128,128]{2,1,0:T(8,128)S(1)}, u32[]{:S(2)}, u32[]{:S(2)}) collective-permute-start(f32[4,128,128]{2,1,0:T(8,128)S(1)} %pad_maximum_fusion.near_ref), channel_id=1, source_target_pairs={{0,1},{1,0},{2,3},{3,2},{4,5},{5,4},{6,7},{7,6},{8,9},{9,8},{10,11... | collective-permute-start | bytes 786440 | tf_op jit(solution)/shard_map/ppermute | solution.py:201
  11.1 31.0 %slice-start.2 = ((s8[8388608]{0:T(1024)(128)(4,1)}), s8[4194304]{0:T(1024)(128)(4,1)S(1)}, s32[]{:S(2)}) async-start(s8[8388608]{0:T(1024)(128)(4,1)} %bitcast.6), calls=%async_computation.3 | async-start | bytes 8388608
  11.1 30.9 %copy-start.1 = (f32[64,64]{1,0:T(8,128)S(1)}, f32[64,64]{1,0:T(8,128)}, u32[]{:S(2)}) copy-start(f32[64,64]{1,0:T(8,128)} %factor_ref.3) | copy-start | bytes 49156
  11.1 30.9 %copy-start.2 = (f32[64,64]{1,0:T(8,128)S(1)}, f32[64,64]{1,0:T(8,128)}, u32[]{:S(2)}) copy-start(f32[64,64]{1,0:T(8,128)} %diag_grad_ref.1) | copy-start | bytes 49156
  11.1 30.9 %copy-start.3 = (f32[4,2048]{1,0:T(4,128)S(1)}, f32[4,2048]{1,0:T(4,128)}, u32[]{:S(2)}) copy-start(f32[4,2048]{1,0:T(4,128)} %row_grad_ref.1) | copy-start | bytes 98308
  12.6 29.5 %slice-start.3 = ((s8[8388608]{0:T(1024)(128)(4,1)}), s8[4194304]{0:T(1024)(128)(4,1)S(1)}, s32[]{:S(2)}) async-start(s8[8388608]{0:T(1024)(128)(4,1)} %bitcast.6), calls=%async_computation.4 | async-start | bytes 8388608

commit v4 on v3

--- a/solution.py
+++ b/solution.py
@@ -57,7 +57,7 @@
         rows_ref[OWN * j : OWN * (j + 1), :] = row_panel_ref[:, 128 * j : 128 * (j + 1)]
 
 
-def solve_line(line_ref, inverse_ref, left_ref):
+def solve_line(line_ref, inverse_ref, left_ref, first):
     grads = jnp.concatenate([line_ref[k, :N, :] for k in range(4)], axis=1)
     panels = jnp.concatenate([line_ref[k, N:, :] for k in range(4)], axis=1)
     solved = dot(inverse_ref[...], grads, (0, 0), HIGHEST)
@@ -69,8 +69,9 @@
     lane = lax.broadcasted_iota(jnp.int32, doubled.shape, 1)
     rounded = doubled.astype(BF16).astype(F32)
     pieces = jnp.where(lane < N, rounded, doubled - rounded).astype(BF16)
-    left_ref[:, : 2 * N] = pieces
-    left_ref[:, 2 * N :] = pieces
+    part = slice(first, first + TILE_ROWS // 2)
+    left_ref[part, : 2 * N] = pieces
+    left_ref[part, 2 * N :] = pieces
     return solved, both, term[:N] + term[N:]
 
 
@@ -82,30 +83,50 @@
 
 
 CHUNK = 256
+HALF = N // 2
+PACKED = 3 * HALF * HALF // 128
+
+
+def pack_lower(term):
+    blocks = jnp.concatenate([term[:HALF, :HALF], term[HALF:, :HALF], term[HALF:, HALF:]], axis=1)
+    rest = jnp.concatenate([blocks[PACKED:, HALF * i : HALF * (i + 1)] for i in range(3)], axis=0)
+    return jnp.concatenate([blocks[:PACKED], rest], axis=1)
+
+
+def unpack_lower(packed):
+    step = HALF - PACKED
+    rest = jnp.concatenate([packed[step * i : step * (i + 1), 3 * HALF :] for i in range(3)], axis=1)
+    blocks = jnp.concatenate([packed[:, : 3 * HALF], rest], axis=0)
+    top = jnp.concatenate([blocks[:, :HALF], jnp.zeros((HALF, HALF), F32)], axis=1)
+    return jnp.concatenate([top, blocks[:, HALF:]], axis=0)
 
 
 def near_kernel(
     near_ref, inverse_ref, tile_ref,
-    own_ref, left_ref, term_ref, part_ref,
-):
-    solved, both, term = solve_line(near_ref, inverse_ref, left_ref)
-    own_ref[...] = solved[:, :LOCAL]
+    own_hbm, left_ref, term_ref, part_ref,
+    own, sem,
+):
+    solved, both, term = solve_line(near_ref, inverse_ref, left_ref, 0)
+    own[...] = solved[:, :LOCAL]
+    copy = pltpu.make_async_copy(own, own_hbm, sem)
+    copy.start()
     term_ref[...] = term
     for i in range(TILE_COLS // CHUNK):
         cols = slice(i * CHUNK, (i + 1) * CHUNK)
         part_ref[:, cols] = line_product(both, tile_ref, cols, False)
+    copy.wait()
 
 
 def far_kernel(
-    far_ref, inverse_ref, rows_ref, tile_ref, near_term_ref, near_part_ref,
+    far_ref, inverse_ref, rows_ref, tile_ref, near_term_ref, near_part_ref, near_left_ref,
     left_ref, send_ref,
 ):
     own_rows = rows_ref[...]
     for s in range(ROWS):
         send_ref[s, N : 2 * N, :] = own_rows
-    _, both, term = solve_line(far_ref, inverse_ref, left_ref)
+    _, both, term = solve_line(far_ref, inverse_ref, left_ref, TILE_ROWS // 2)
     term = term + near_term_ref[...]
-    packed = jnp.concatenate([term[: N // 2], term[N // 2 :]], axis=1)
+    packed = pack_lower(term)
     for s in range(ROWS):
         send_ref[s, 2 * N :, :] = packed
     for i in range(TILE_COLS // CHUNK):
@@ -118,35 +139,37 @@
 
 
 def update_kernel(
-    recv_ref, near_left_ref, far_left_ref, inverse_ref, factor_ref, diag_grad_ref, row_grad_ref, grad_ref,
-    out_ref, row_out_ref, diag_out_ref,
-    result, full, right, small, out_sems,
-):
-    for s in range(ROWS):
-        for j in range(PIECES):
-            full[OWN * s : OWN * (s + 1), 128 * j : 128 * (j + 1)] = recv_ref[s, N + OWN * j : N + OWN * (j + 1), :]
-    high, low = split(full[...])
-    right[:N] = high
-    right[N : 2 * N] = high
-    right[2 * N : 3 * N] = low
-    right[3 * N :] = low
+    recv_ref, left, inverse_ref, factor_ref, diag_grad_ref, row_grad_ref, grad_ref,
+    out_ref, row_out_hbm, diag_out_hbm,
+    result, full, right, small, row_out, diag_out, out_sems, small_sems,
+):
     stores = []
-
-    def step(left_ref, k, other):
-        part = pl.ds(block_row(k, other), LOCAL)
-        result[part] = grad_ref[part] - dot(left_ref[k * LOCAL : (k + 1) * LOCAL], right[...], (1, 0))
-        stores.append(pltpu.make_async_copy(result.at[part], out_ref.at[part], out_sems.at[len(stores)]))
+    edges = [0, 256, 512, 768, 1024, 1280, 1536, 1792, 2048]
+
+    def step(i):
+        cols = slice(edges[i], edges[i + 1])
+        for s in range(ROWS):
+            for j in range(edges[i] // 128, edges[i + 1] // 128):
+                full[OWN * s : OWN * (s + 1), 128 * j : 128 * (j + 1)] = recv_ref[s, N + OWN * j : N + OWN * (j + 1), :]
+        high, low = split(full[:, cols])
+        right[:, cols] = jnp.concatenate([high, high, low, low], axis=0)
+        product = dot(left[...], right[:, cols], (1, 0))
+        for slot in range(COLS):
+            part = pl.ds(block_row(slot % 4, slot >= 4), LOCAL)
+            result[part, cols] = grad_ref[part, cols] - product[slot * LOCAL : (slot + 1) * LOCAL]
+        stores.append(pltpu.make_async_copy(result.at[:, cols], out_ref.at[:, cols], out_sems.at[i]))
         stores[-1].start()
 
-    for k in range(4):
-        step(near_left_ref, k, False)
+    count = len(edges) - 1
+    for i in range(4):
+        step(i)
 
     packed = recv_ref[0, 2 * N :, :]
     reduced = recv_ref[0, :N, :]
     for s in range(1, ROWS):
         packed = packed + recv_ref[s, 2 * N :, :]
         reduced = reduced + recv_ref[s, :N, :]
-    total = jnp.concatenate([packed[:, :N], packed[:, N:]], axis=0)
+    total = unpack_lower(packed)
     inverse, factor = inverse_ref[...], factor_ref[...]
     r_id = lax.broadcasted_iota(jnp.int32, (N, N), 0)
     c_id = lax.broadcasted_iota(jnp.int32, (N, N), 1)
@@ -156,18 +179,22 @@
     phi = jnp.where(r_id == c_id, 0.5 * phi, phi)
     spart = dot(dot(inverse, phi, (0, 0), HIGHEST), inverse, (1, 0), HIGHEST)
     both = spart + spart.T
-    diag_out_ref[...] = 0.5 * both
+    diag_out[...] = 0.5 * both
+    stores.append(pltpu.make_async_copy(diag_out, diag_out_hbm, small_sems.at[0]))
+    stores[-1].start()
     small[...] = both
     own_both = small[pl.ds(lax.axis_index("row") * OWN, OWN), :]
     both_high, both_low = split(own_both)
     wide = jnp.concatenate([both_high, both_low, both_high, both_low], axis=1)
+
+    for i in range(4, count):
+        step(i)
     second = dot(wide, right[...], (1, 0))
     for j in range(PIECES):
         cols = slice(128 * j, 128 * (j + 1))
-        row_out_ref[:, cols] = row_grad_ref[:, cols] - reduced[OWN * j : OWN * (j + 1), :] - second[:, cols]
-
-    for k in range(4):
-        step(far_left_ref, k, True)
+        row_out[:, cols] = row_grad_ref[:, cols] - reduced[OWN * j : OWN * (j + 1), :] - second[:, cols]
+    stores.append(pltpu.make_async_copy(row_out, row_out_hbm, small_sems.at[1]))
+    stores[-1].start()
     for copy in stores:
         copy.wait()
 
@@ -199,31 +226,33 @@
     )(payload, diag_factor, row_panel)
     near = jnp.stack([payload, right, opposite, left])
     far = lax.ppermute(near, "col", [(i, i ^ 1) for i in range(COLS)])
-    panel_out, near_left, near_term, near_part = pl.pallas_call(
+    panel_out, left_factor, near_term, near_part = pl.pallas_call(
         near_kernel,
         out_shape=(
             jax.ShapeDtypeStruct((N, LOCAL), F32),
-            jax.ShapeDtypeStruct((TILE_ROWS // 2, 4 * N), BF16),
+            jax.ShapeDtypeStruct((TILE_ROWS, 4 * N), BF16),
             jax.ShapeDtypeStruct((N, N), F32),
             jax.ShapeDtypeStruct((N, TILE_COLS), F32),
         ),
         in_specs=[vmem] * 3,
-        out_specs=(vmem,) * 4,
+        out_specs=(anywhere,) + (vmem,) * 3,
+        scratch_shapes=[pltpu.VMEM((N, LOCAL), F32), pltpu.SemaphoreType.DMA],
         compiler_params=pltpu.CompilerParams(vmem_limit_bytes=16 * MIB),
         cost_estimate=pl.CostEstimate(flops=1_000_000_000, bytes_accessed=0, transcendentals=0),
         name="near",
     )(near, inverse, trailing)
-    far_left, send = pl.pallas_call(
+    left_factor, send = pl.pallas_call(
         far_kernel,
         out_shape=(
-            jax.ShapeDtypeStruct((TILE_ROWS // 2, 4 * N), BF16),
-            jax.ShapeDtypeStruct((ROWS, 2 * N + N // 2, 128), F32),
-        ),
-        in_specs=[vmem] * 6,
+            jax.ShapeDtypeStruct((TILE_ROWS, 4 * N), BF16),
+            jax.ShapeDtypeStruct((ROWS, 2 * N + PACKED, 128), F32),
+        ),
+        in_specs=[vmem] * 6 + [anywhere],
         out_specs=(vmem,) * 2,
+        input_output_aliases={6: 0},
         compiler_params=pltpu.CompilerParams(vmem_limit_bytes=16 * MIB),
         name="far",
-    )(far, inverse, rows, trailing, near_term, near_part)
+    )(far, inverse, rows, trailing, near_term, near_part, left_factor)
     recv = lax.all_to_all(send, "row", 0, 0)
     trailing_out, row_out, diag_out = pl.pallas_call(
         update_kernel,
@@ -232,18 +261,21 @@
             jax.ShapeDtypeStruct((OWN, TILE_COLS), F32),
             jax.ShapeDtypeStruct((N, N), F32),
         ),
-        in_specs=[vmem] * 8,
-        out_specs=(anywhere, vmem, vmem),
+        in_specs=[vmem] * 7,
+        out_specs=(anywhere,) * 3,
         scratch_shapes=[
             pltpu.VMEM((TILE_ROWS, TILE_COLS), F32),
             pltpu.VMEM((N, TILE_COLS), F32),
             pltpu.VMEM((4 * N, TILE_COLS), BF16),
             pltpu.VMEM((N, N), F32),
+            pltpu.VMEM((OWN, TILE_COLS), F32),
+            pltpu.VMEM((N, N), F32),
             pltpu.SemaphoreType.DMA((8,)),
+            pltpu.SemaphoreType.DMA((2,)),
         ],
         compiler_params=pltpu.CompilerParams(vmem_limit_bytes=32 * MIB),
         name="update",
-    )(recv, near_left, far_left, inverse, diag_factor, diag_grad, row_grad, trailing_grad)
+    )(recv, left_factor, inverse, diag_factor, diag_grad, row_grad, trailing_grad)
     return (panel_out, trailing_out, row_out, diag_out)
 
 

time: 46.7 us -> 45.4 us (0.972)
  Pallas kernels: 7.89 us -> 7.06 us
  blocking collectives: 28.2 us -> 27.4 us
    all_to_all x1, blocking collectives: 28.2 us -> 27.4 us  [per_device(): recv = lax.all_to_all(send, 'row', 0, 0)]
    pallas_call x1, Pallas kernels: 4.39 us -> 3.91 us  [per_device(): pl.pallas_call(update_kernel, out_shape=(jax.ShapeDtypeStruct((TILE_ROWS,...]
  transfers between devices with their start and end apart: 4 -> 4, of which waited for: 2 -> 3; matrix products, arithmetic and copies ran while one was open for 0% -> 0% of each run, Pallas kernels for 5% -> 4%
where the time goes in v4:
time: 45.4 us; the launch traced here: 45.1 us
  blocking collectives  27.4 us (60%)
  Pallas kernels  7.06 us (16%)
  starting transfers between devices  4.67 us (10%)
  waiting for transfers between devices  2.73 us (6%)
  local copies, waits for them, and re-layouts  1.56 us (3%)
  other arithmetic  0.95 us (2%)
  between operations  0.77 us (2%)
    all_to_all x1, blocking collectives, per_device(): recv = lax.all_to_all(send, 'row', 0, 0)  27.4 us
    ppermute x3, starting transfers between devices, across_chips(): return lax.ppermute(value, 'col', pairs)  4.58 us
    pallas_call x1, Pallas kernels, per_device(): pl.pallas_call(update_kernel, out_shape=(jax.ShapeDtypeStruct((TILE_ROWS,...  3.91 us
    ppermute x3, waiting for transfers between devices, across_chips(): return lax.ppermute(value, 'col', pairs)  2.42 us
    unnamed x18, local copies, waits for them, and re-layouts  1.56 us
    pallas_call x1, Pallas kernels, per_device(): pl.pallas_call(far_kernel, out_shape=(jax.ShapeDtypeStruct((TILE_ROWS, 4...  1.19 us
    pallas_call x1, Pallas kernels, per_device(): pl.pallas_call(near_kernel, out_shape=(jax.ShapeDtypeStruct((N, LOCAL), F...  1.12 us
    add x1, other arithmetic, per_device(): jnp.pad(panel_grad_t, ((0, N), (0, 0))) + jnp.pad(panel_t, ((N, 0), (0, 0)))  0.93 us
  transfers between devices with their start and end apart: 4, of which 3 were waited for; matrix products, arithmetic and copies ran while one was open for 0% of the time, Pallas kernels for 4%

profile of v4, /device:TPU:0, one launch (start us, length us, event | category | flops | bytes accessed | tf_op | source)
XLA Modules:
  0.0 45.1 jit_solution(14880274907318857945)
XLA Ops:
  0.6 0.0 slice-start
  0.6 0.9 %pad_add_fusion.payload_ref = f32[128,128]{1,0:T(8,128)S(1)} fusion(f32[64,128]{1,0:T(8,128)} %param.8, f32[64,128]{1,0:T(8,128)} %param.9), kind=kLoop, calls=%fused_computation.1 | loop fusion | flops 16384 | bytes 131072 | tf_op jit(solution)/shard_map/add | solution.py:210
  1.6 0.0 slice-start.1
  1.6 2.9 %collective-permute-start.2 = (f32[128,128]{1,0:T(8,128)S(1)}, f32[128,128]{1,0:T(8,128)S(1)}, u32[]{:S(2)}, u32[]{:S(2)}) collective-permute-start(f32[128,128]{1,0:T(8,128)S(1)} %pad_add_fusion.payload_ref), channel_id=1, source_target_pairs={{0,6},{1,7},{2,0},{3,1},{4,2},{5,3},{6,4},{7,5},{8,14},{9,15},{10,... | collective-permute-start | bytes 196616 | tf_op jit(solution)/shard_map/ppermute | solution.py:204
  4.5 0.8 %collective-permute-start.1 = (f32[128,128]{1,0:T(8,128)S(1)}, f32[128,128]{1,0:T(8,128)S(1)}, u32[]{:S(2)}, u32[]{:S(2)}) collective-permute-start(f32[128,128]{1,0:T(8,128)S(1)} %pad_add_fusion.payload_ref), channel_id=1, source_target_pairs={{0,4},{1,5},{2,6},{3,7},{4,0},{5,1},{6,2},{7,3},{8,12},{9,13},{10,... | collective-permute-start | bytes 196616 | tf_op jit(solution)/shard_map/ppermute | solution.py:204
  5.3 0.9 %collective-permute-start = (f32[128,128]{1,0:T(8,128)S(1)}, f32[128,128]{1,0:T(8,128)S(1)}, u32[]{:S(2)}, u32[]{:S(2)}) collective-permute-start(f32[128,128]{1,0:T(8,128)S(1)} %pad_add_fusion.payload_ref), channel_id=1, source_target_pairs={{0,2},{1,3},{2,4},{3,5},{4,6},{5,7},{6,0},{7,1},{8,10},{9,11},{10,... | collective-permute-start | bytes 196616 | tf_op jit(solution)/shard_map/ppermute | solution.py:204
  6.2 0.0 copy-start
  6.2 0.8 %copy-done = f32[64,64]{1,0:T(8,128)S(1)} copy-done((f32[64,64]{1,0:T(8,128)S(1)}, f32[64,64]{1,0:T(8,128)}, u32[]{:S(2)}) %copy-start) | copy-done | bytes 16408
  6.9 0.0 copy-start.4
  6.9 0.8 %copy-done.4 = f32[4,2048]{1,0:T(4,128)S(1)} copy-done((f32[4,2048]{1,0:T(4,128)S(1)}, f32[4,2048]{1,0:T(4,128)}, u32[]{:S(2)}) %copy-start.4) | copy-done | bytes 32792
  7.7 0.8 %prepare.1 = (f32[64,64]{1,0:T(8,128)S(1)}, f32[128,128]{1,0:T(8,128)S(1)}, f32[64,128]{1,0:T(8,128)S(1)}) custom-call(f32[128,128]{1,0:T(8,128)S(1)} %pad_add_fusion.payload_ref, f32[64,64]{1,0:T(8,128)S(1)} %copy-done, f32[4,2048]{1,0:T(4,128)S(1)} %copy-done.4), custom_call_target="tpu_custom_call" | custom-call | flops 4000000000 | tf_op jit(solution)/shard_map/prepare/pallas_call | solution.py:214
  8.5 0.0 collective-permute-done.2
  8.5 1.7 %collective-permute-done.1 = f32[128,128]{1,0:T(8,128)S(1)} collective-permute-done((f32[128,128]{1,0:T(8,128)S(1)}, f32[128,128]{1,0:T(8,128)S(1)}, u32[]{:S(2)}, u32[]{:S(2)}) %collective-permute-start.1) | collective-permute-done | bytes 65568 | tf_op jit(solution)/shard_map/ppermute | solution.py:204
  10.3 0.7 %collective-permute-done = f32[128,128]{1,0:T(8,128)S(1)} collective-permute-done((f32[128,128]{1,0:T(8,128)S(1)}, f32[128,128]{1,0:T(8,128)S(1)}, u32[]{:S(2)}, u32[]{:S(2)}) %collective-permute-start) | collective-permute-done | bytes 65568 | tf_op jit(solution)/shard_map/ppermute | solution.py:204
  11.0 0.1 collective-permute-start.3
  11.1 0.0 slice-done
  11.1 0.0 slice-done.1
  11.1 0.0 slice-start.2
  11.1 0.0 copy-start.1
  11.1 0.0 copy-start.2
  11.1 0.0 copy-start.3
  11.1 1.1 %near.1 = (f32[64,128]{1,0:T(8,128)}, bf16[1024,256]{1,0:T(8,128)(2,1)S(1)}, f32[64,64]{1,0:T(8,128)S(1)}, f32[64,2048]{1,0:T(8,128)S(1)}) custom-call(f32[4,128,128]{2,1,0:T(8,128)S(1)} %pad_maximum_fusion.near_ref, f32[64,64]{1,0:T(8,128)S(1)} %get-tuple-element.17.inverse_ref, f32[1024,2048]{1,0:T(8,128)S(1)} %bitcast.5), custom_call_target="tpu_custom_call" | custom-call | flops 1000000000 | tf_op jit(solution)/shard_map/near/pallas_call | solution.py:229
  12.3 0.3 collective-permute-done.3.far_ref
  12.6 0.0 slice-start.3
  12.6 1.2 %far.1 = (bf16[1024,256]{1,0:T(8,128)(2,1)S(1)}, f32[16,152,128]{2,1,0:T(8,128)S(1)}) custom-call(f32[4,128,128]{2,1,0:T(8,128)S(1)} %collective-permute-done.3.far_ref, f32[64,64]{1,0:T(8,128)S(1)} %get-tuple-element.17.inverse_ref, f32[64,128]{1,0:T(8,128)S(1)} %get-tuple-element.19.rows_ref, ...), custom_call_target="tpu_custom_call", output_to_operand_aliasing={{0}: (6, {})} | custom-call | tf_op jit(solution)/shard_map/far/pallas_call | solution.py:244
  13.8 27.4 %all_to_all.5.recv_ref = f32[16,152,128]{2,1,0:T(8,128)S(1)} all-to-all(f32[16,152,128]{2,1,0:T(8,128)S(1)} %get-tuple-element.23), channel_id=1, replica_groups=mesh['row'=16,'col'=8] {'row'}, dimensions={0} | all-to-all | bytes 2490368 | tf_op jit(solution)/shard_map/all_to_all | solution.py:256
  41.2 0.0 slice-done.2
  41.2 0.0 copy-done.1
  41.2 0.0 copy-done.2
  41.2 0.0 copy-done.3
  41.2 0.0 slice-done.3
  41.2 3.9 %update.1 = (f32[1024,2048]{1,0:T(8,128)}, f32[4,2048]{1,0:T(4,128)}, f32[64,64]{1,0:T(8,128)}) custom-call(f32[16,152,128]{2,1,0:T(8,128)S(1)} %all_to_all.5.recv_ref, bf16[1024,256]{1,0:T(8,128)(2,1)S(1)} %get-tuple-element.24.left, f32[64,64]{1,0:T(8,128)S(1)} %get-tuple-element.17.inverse_ref, f32[64,64]{1,0:T(8,128)S(1)} %copy-done.1, ...), custom_call_target="tpu_custom_call" | custom-call | tf_op jit(solution)/shard_map/update/pallas_call | solution.py:257
  (3 shorter events, 0.0 us)
Async XLA Ops:
  0.6 10.4 %slice-start = ((s8[8388608]{0:T(1024)(128)(4,1)}), s8[4194304]{0:T(1024)(128)(4,1)S(1)}, s32[]{:S(2)}) async-start(s8[8388608]{0:T(1024)(128)(4,1)} %bitcast.4), calls=%async_computation.1 | async-start | bytes 8388608
  1.6 9.5 %slice-start.1 = ((s8[8388608]{0:T(1024)(128)(4,1)}), s8[4194304]{0:T(1024)(128)(4,1)S(1)}, s32[]{:S(2)}) async-start(s8[8388608]{0:T(1024)(128)(4,1)} %bitcast.4), calls=%async_computation.2 | async-start | bytes 8388608
  1.6 6.9 %collective-permute-start.2 = (f32[128,128]{1,0:T(8,128)S(1)}, f32[128,128]{1,0:T(8,128)S(1)}, u32[]{:S(2)}, u32[]{:S(2)}) collective-permute-start(f32[128,128]{1,0:T(8,128)S(1)} %pad_add_fusion.payload_ref), channel_id=1, source_target_pairs={{0,6},{1,7},{2,0},{3,1},{4,2},{5,3},{6,4},{7,5},{8,14},{9,15},{10,... | collective-permute-start | bytes 196616 | tf_op jit(solution)/shard_map/ppermute | solution.py:204
  4.5 5.8 %collective-permute-start.1 = (f32[128,128]{1,0:T(8,128)S(1)}, f32[128,128]{1,0:T(8,128)S(1)}, u32[]{:S(2)}, u32[]{:S(2)}) collective-permute-start(f32[128,128]{1,0:T(8,128)S(1)} %pad_add_fusion.payload_ref), channel_id=1, source_target_pairs={{0,4},{1,5},{2,6},{3,7},{4,0},{5,1},{6,2},{7,3},{8,12},{9,13},{10,... | collective-permute-start | bytes 196616 | tf_op jit(solution)/shard_map/ppermute | solution.py:204
  5.3 5.7 %collective-permute-start = (f32[128,128]{1,0:T(8,128)S(1)}, f32[128,128]{1,0:T(8,128)S(1)}, u32[]{:S(2)}, u32[]{:S(2)}) collective-permute-start(f32[128,128]{1,0:T(8,128)S(1)} %pad_add_fusion.payload_ref), channel_id=1, source_target_pairs={{0,2},{1,3},{2,4},{3,5},{4,6},{5,7},{6,0},{7,1},{8,10},{9,11},{10,... | collective-permute-start | bytes 196616 | tf_op jit(solution)/shard_map/ppermute | solution.py:204
  6.2 0.8 %copy-start = (f32[64,64]{1,0:T(8,128)S(1)}, f32[64,64]{1,0:T(8,128)}, u32[]{:S(2)}) copy-start(f32[64,64]{1,0:T(8,128)} %factor_ref.3) | copy-start | bytes 49156
  6.9 0.8 %copy-start.4 = (f32[4,2048]{1,0:T(4,128)S(1)}, f32[4,2048]{1,0:T(4,128)}, u32[]{:S(2)}) copy-start(f32[4,2048]{1,0:T(4,128)} %row_panel_ref.1) | copy-start | bytes 98308
  11.0 1.6 %collective-permute-start.3 = (f32[4,128,128]{2,1,0:T(8,128)S(1)}, f32[4,128,128]{2,1,0:T(8,128)S(1)}, u32[]{:S(2)}, u32[]{:S(2)}) collective-permute-start(f32[4,128,128]{2,1,0:T(8,128)S(1)} %pad_maximum_fusion.near_ref), channel_id=1, source_target_pairs={{0,1},{1,0},{2,3},{3,2},{4,5},{5,4},{6,7},{7,6},{8,9},{9,8},{10,11... | collective-permute-start | bytes 786440 | tf_op jit(solution)/shard_map/ppermute | solution.py:228
  11.1 30.1 %slice-start.2 = ((s8[8388608]{0:T(1024)(128)(4,1)}), s8[4194304]{0:T(1024)(128)(4,1)S(1)}, s32[]{:S(2)}) async-start(s8[8388608]{0:T(1024)(128)(4,1)} %bitcast.6), calls=%async_computation.3 | async-start | bytes 8388608
  11.1 30.1 %copy-start.1 = (f32[64,64]{1,0:T(8,128)S(1)}, f32[64,64]{1,0:T(8,128)}, u32[]{:S(2)}) copy-start(f32[64,64]{1,0:T(8,128)} %factor_ref.3) | copy-start | bytes 49156
  11.1 30.1 %copy-start.2 = (f32[64,64]{1,0:T(8,128)S(1)}, f32[64,64]{1,0:T(8,128)}, u32[]{:S(2)}) copy-start(f32[64,64]{1,0:T(8,128)} %diag_grad_ref.1) | copy-start | bytes 49156
  11.1 30.0 %copy-start.3 = (f32[4,2048]{1,0:T(4,128)S(1)}, f32[4,2048]{1,0:T(4,128)}, u32[]{:S(2)}) copy-start(f32[4,2048]{1,0:T(4,128)} %row_grad_ref.1) | copy-start | bytes 98308
  12.6 28.6 %slice-start.3 = ((s8[8388608]{0:T(1024)(128)(4,1)}), s8[4194304]{0:T(1024)(128)(4,1)S(1)}, s32[]{:S(2)}) async-start(s8[8388608]{0:T(1024)(128)(4,1)} %bitcast.6), calls=%async_computation.4 | async-start | bytes 8388608

commit v5 on v4

--- a/solution.py
+++ b/solution.py
@@ -13,6 +13,8 @@
 TILE_COLS = 2048
 OWN = N // ROWS
 PIECES = TILE_COLS // 128
+ORDER = [15, 14, 13, 12, 11, 10, 9, 8, 7, 6, 5, 4, 3, 2, 1, 0]
+SLOT = [15, 14, 13, 12, 11, 10, 9, 8, 7, 6, 5, 4, 3, 2, 1, 0]
 HIGHEST = lax.Precision.HIGHEST
 F32 = jnp.float32
 BF16 = jnp.bfloat16
@@ -135,7 +137,7 @@
         for s in range(ROWS):
             for jj in range(CHUNK // 128):
                 j = i * (CHUNK // 128) + jj
-                send_ref[s, OWN * j : OWN * (j + 1), :] = part[OWN * s : OWN * (s + 1), 128 * jj : 128 * (jj + 1)]
+                send_ref[SLOT[s], OWN * j : OWN * (j + 1), :] = part[OWN * s : OWN * (s + 1), 128 * jj : 128 * (jj + 1)]
 
 
 def update_kernel(
@@ -150,7 +152,7 @@
         cols = slice(edges[i], edges[i + 1])
         for s in range(ROWS):
             for j in range(edges[i] // 128, edges[i + 1] // 128):
-                full[OWN * s : OWN * (s + 1), 128 * j : 128 * (j + 1)] = recv_ref[s, N + OWN * j : N + OWN * (j + 1), :]
+                full[OWN * s : OWN * (s + 1), 128 * j : 128 * (j + 1)] = recv_ref[SLOT[s], N + OWN * j : N + OWN * (j + 1), :]
         high, low = split(full[:, cols])
         right[:, cols] = jnp.concatenate([high, high, low, low], axis=0)
         product = dot(left[...], right[:, cols], (1, 0))
@@ -253,7 +255,7 @@
         compiler_params=pltpu.CompilerParams(vmem_limit_bytes=16 * MIB),
         name="far",
     )(far, inverse, rows, trailing, near_term, near_part, left_factor)
-    recv = lax.all_to_all(send, "row", 0, 0)
+    recv = lax.all_to_all(send, "row", 0, 0, axis_index_groups=[ORDER])
     trailing_out, row_out, diag_out = pl.pallas_call(
         update_kernel,
         out_shape=(

time: 45.4 us -> 43 us (0.947)
  blocking collectives: 27.4 us -> 24.9 us
    all_to_all x1, blocking collectives: 27.4 us -> 24.9 us  [per_device(): recv = lax.all_to_all(send, 'row', 0, 0, axis_index_groups=[ORDER])]
  transfers between devices with their start and end apart: 4 -> 4, of which waited for: 3 -> 3; matrix products, arithmetic and copies ran while one was open for 0% -> 0% of each run, Pallas kernels for 4% -> 5%
where the time goes in v5:
time: 43 us; the launch traced here: 42.6 us
  blocking collectives  24.9 us (58%)
  Pallas kernels  7.06 us (16%)
  starting transfers between devices  4.67 us (11%)
  waiting for transfers between devices  2.73 us (6%)
  local copies, waits for them, and re-layouts  1.56 us (4%)
  other arithmetic  0.95 us (2%)
  between operations  0.77 us (2%)
    all_to_all x1, blocking collectives, per_device(): recv = lax.all_to_all(send, 'row', 0, 0, axis_index_groups=[ORDER])  24.9 us
    ppermute x3, starting transfers between devices, across_chips(): return lax.ppermute(value, 'col', pairs)  4.58 us
    pallas_call x1, Pallas kernels, per_device(): pl.pallas_call(update_kernel, out_shape=(jax.ShapeDtypeStruct((TILE_ROWS,...  3.91 us
    ppermute x3, waiting for transfers between devices, across_chips(): return lax.ppermute(value, 'col', pairs)  2.42 us
    unnamed x18, local copies, waits for them, and re-layouts  1.56 us
    pallas_call x1, Pallas kernels, per_device(): pl.pallas_call(far_kernel, out_shape=(jax.ShapeDtypeStruct((TILE_ROWS, 4...  1.19 us
    pallas_call x1, Pallas kernels, per_device(): pl.pallas_call(near_kernel, out_shape=(jax.ShapeDtypeStruct((N, LOCAL), F...  1.12 us
    add x1, other arithmetic, per_device(): jnp.pad(panel_grad_t, ((0, N), (0, 0))) + jnp.pad(panel_t, ((N, 0), (0, 0)))  0.93 us
  transfers between devices with their start and end apart: 4, of which 3 were waited for; matrix products, arithmetic and copies ran while one was open for 0% of the time, Pallas kernels for 5%

profile of v5, /device:TPU:0, one launch (start us, length us, event | category | flops | bytes accessed | tf_op | source)
XLA Modules:
  0.0 42.6 jit_solution(5830442264364177164)
XLA Ops:
  0.6 0.0 slice-start
  0.6 0.9 %pad_add_fusion.payload_ref = f32[128,128]{1,0:T(8,128)S(1)} fusion(f32[64,128]{1,0:T(8,128)} %param.8, f32[64,128]{1,0:T(8,128)} %param.9), kind=kLoop, calls=%fused_computation.1 | loop fusion | flops 16384 | bytes 131072 | tf_op jit(solution)/shard_map/add | solution.py:212
  1.6 0.0 slice-start.1
  1.6 2.9 %collective-permute-start.2 = (f32[128,128]{1,0:T(8,128)S(1)}, f32[128,128]{1,0:T(8,128)S(1)}, u32[]{:S(2)}, u32[]{:S(2)}) collective-permute-start(f32[128,128]{1,0:T(8,128)S(1)} %pad_add_fusion.payload_ref), channel_id=1, source_target_pairs={{0,6},{1,7},{2,0},{3,1},{4,2},{5,3},{6,4},{7,5},{8,14},{9,15},{10,... | collective-permute-start | bytes 196616 | tf_op jit(solution)/shard_map/ppermute | solution.py:206
  4.5 0.8 %collective-permute-start.1 = (f32[128,128]{1,0:T(8,128)S(1)}, f32[128,128]{1,0:T(8,128)S(1)}, u32[]{:S(2)}, u32[]{:S(2)}) collective-permute-start(f32[128,128]{1,0:T(8,128)S(1)} %pad_add_fusion.payload_ref), channel_id=1, source_target_pairs={{0,4},{1,5},{2,6},{3,7},{4,0},{5,1},{6,2},{7,3},{8,12},{9,13},{10,... | collective-permute-start | bytes 196616 | tf_op jit(solution)/shard_map/ppermute | solution.py:206
  5.3 0.9 %collective-permute-start = (f32[128,128]{1,0:T(8,128)S(1)}, f32[128,128]{1,0:T(8,128)S(1)}, u32[]{:S(2)}, u32[]{:S(2)}) collective-permute-start(f32[128,128]{1,0:T(8,128)S(1)} %pad_add_fusion.payload_ref), channel_id=1, source_target_pairs={{0,2},{1,3},{2,4},{3,5},{4,6},{5,7},{6,0},{7,1},{8,10},{9,11},{10,... | collective-permute-start | bytes 196616 | tf_op jit(solution)/shard_map/ppermute | solution.py:206
  6.2 0.0 copy-start
  6.2 0.8 %copy-done = f32[64,64]{1,0:T(8,128)S(1)} copy-done((f32[64,64]{1,0:T(8,128)S(1)}, f32[64,64]{1,0:T(8,128)}, u32[]{:S(2)}) %copy-start) | copy-done | bytes 16408
  6.9 0.0 copy-start.4
  6.9 0.8 %copy-done.4 = f32[4,2048]{1,0:T(4,128)S(1)} copy-done((f32[4,2048]{1,0:T(4,128)S(1)}, f32[4,2048]{1,0:T(4,128)}, u32[]{:S(2)}) %copy-start.4) | copy-done | bytes 32792
  7.7 0.8 %prepare.1 = (f32[64,64]{1,0:T(8,128)S(1)}, f32[128,128]{1,0:T(8,128)S(1)}, f32[64,128]{1,0:T(8,128)S(1)}) custom-call(f32[128,128]{1,0:T(8,128)S(1)} %pad_add_fusion.payload_ref, f32[64,64]{1,0:T(8,128)S(1)} %copy-done, f32[4,2048]{1,0:T(4,128)S(1)} %copy-done.4), custom_call_target="tpu_custom_call" | custom-call | flops 4000000000 | tf_op jit(solution)/shard_map/prepare/pallas_call | solution.py:216
  8.5 0.0 collective-permute-done.2
  8.5 1.7 %collective-permute-done.1 = f32[128,128]{1,0:T(8,128)S(1)} collective-permute-done((f32[128,128]{1,0:T(8,128)S(1)}, f32[128,128]{1,0:T(8,128)S(1)}, u32[]{:S(2)}, u32[]{:S(2)}) %collective-permute-start.1) | collective-permute-done | bytes 65568 | tf_op jit(solution)/shard_map/ppermute | solution.py:206
  10.3 0.7 %collective-permute-done = f32[128,128]{1,0:T(8,128)S(1)} collective-permute-done((f32[128,128]{1,0:T(8,128)S(1)}, f32[128,128]{1,0:T(8,128)S(1)}, u32[]{:S(2)}, u32[]{:S(2)}) %collective-permute-start) | collective-permute-done | bytes 65568 | tf_op jit(solution)/shard_map/ppermute | solution.py:206
  11.0 0.1 collective-permute-start.3
  11.1 0.0 slice-done
  11.1 0.0 slice-done.1
  11.1 0.0 slice-start.2
  11.1 0.0 copy-start.1
  11.1 0.0 copy-start.2
  11.1 0.0 copy-start.3
  11.1 1.1 %near.1 = (f32[64,128]{1,0:T(8,128)}, bf16[1024,256]{1,0:T(8,128)(2,1)S(1)}, f32[64,64]{1,0:T(8,128)S(1)}, f32[64,2048]{1,0:T(8,128)S(1)}) custom-call(f32[4,128,128]{2,1,0:T(8,128)S(1)} %pad_maximum_fusion.near_ref, f32[64,64]{1,0:T(8,128)S(1)} %get-tuple-element.17.inverse_ref, f32[1024,2048]{1,0:T(8,128)S(1)} %bitcast.5), custom_call_target="tpu_custom_call" | custom-call | flops 1000000000 | tf_op jit(solution)/shard_map/near/pallas_call | solution.py:231
  12.3 0.3 collective-permute-done.3.far_ref
  12.6 0.0 slice-start.3
  12.6 1.2 %far.1 = (bf16[1024,256]{1,0:T(8,128)(2,1)S(1)}, f32[16,152,128]{2,1,0:T(8,128)S(1)}) custom-call(f32[4,128,128]{2,1,0:T(8,128)S(1)} %collective-permute-done.3.far_ref, f32[64,64]{1,0:T(8,128)S(1)} %get-tuple-element.17.inverse_ref, f32[64,128]{1,0:T(8,128)S(1)} %get-tuple-element.19.rows_ref, ...), custom_call_target="tpu_custom_call", output_to_operand_aliasing={{0}: (6, {})} | custom-call | tf_op jit(solution)/shard_map/far/pallas_call | solution.py:246
  13.8 24.9 %all_to_all.5.recv_ref = f32[16,152,128]{2,1,0:T(8,128)S(1)} all-to-all(f32[16,152,128]{2,1,0:T(8,128)S(1)} %get-tuple-element.23), channel_id=1, replica_groups={{120,112,104,96,88,80,72,64,56,48,40,32,24,16,8,0},{121,113,105,97,89,8..., dimensions={0} | all-to-all | bytes 2490368 | tf_op jit(solution)/shard_map/all_to_all | solution.py:258
  38.6 0.0 slice-done.2
  38.7 0.0 copy-done.1
  38.7 0.0 copy-done.2
  38.7 0.0 copy-done.3
  38.7 0.0 slice-done.3
  38.7 3.9 %update.1 = (f32[1024,2048]{1,0:T(8,128)}, f32[4,2048]{1,0:T(4,128)}, f32[64,64]{1,0:T(8,128)}) custom-call(f32[16,152,128]{2,1,0:T(8,128)S(1)} %all_to_all.5.recv_ref, bf16[1024,256]{1,0:T(8,128)(2,1)S(1)} %get-tuple-element.24.left, f32[64,64]{1,0:T(8,128)S(1)} %get-tuple-element.17.inverse_ref, f32[64,64]{1,0:T(8,128)S(1)} %copy-done.1, ...), custom_call_target="tpu_custom_call" | custom-call | tf_op jit(solution)/shard_map/update/pallas_call | solution.py:259
  (3 shorter events, 0.0 us)
Async XLA Ops:
  0.6 10.4 %slice-start = ((s8[8388608]{0:T(1024)(128)(4,1)}), s8[4194304]{0:T(1024)(128)(4,1)S(1)}, s32[]{:S(2)}) async-start(s8[8388608]{0:T(1024)(128)(4,1)} %bitcast.4), calls=%async_computation.1 | async-start | bytes 8388608
  1.6 9.5 %slice-start.1 = ((s8[8388608]{0:T(1024)(128)(4,1)}), s8[4194304]{0:T(1024)(128)(4,1)S(1)}, s32[]{:S(2)}) async-start(s8[8388608]{0:T(1024)(128)(4,1)} %bitcast.4), calls=%async_computation.2 | async-start | bytes 8388608
  1.6 6.9 %collective-permute-start.2 = (f32[128,128]{1,0:T(8,128)S(1)}, f32[128,128]{1,0:T(8,128)S(1)}, u32[]{:S(2)}, u32[]{:S(2)}) collective-permute-start(f32[128,128]{1,0:T(8,128)S(1)} %pad_add_fusion.payload_ref), channel_id=1, source_target_pairs={{0,6},{1,7},{2,0},{3,1},{4,2},{5,3},{6,4},{7,5},{8,14},{9,15},{10,... | collective-permute-start | bytes 196616 | tf_op jit(solution)/shard_map/ppermute | solution.py:206
  4.5 5.8 %collective-permute-start.1 = (f32[128,128]{1,0:T(8,128)S(1)}, f32[128,128]{1,0:T(8,128)S(1)}, u32[]{:S(2)}, u32[]{:S(2)}) collective-permute-start(f32[128,128]{1,0:T(8,128)S(1)} %pad_add_fusion.payload_ref), channel_id=1, source_target_pairs={{0,4},{1,5},{2,6},{3,7},{4,0},{5,1},{6,2},{7,3},{8,12},{9,13},{10,... | collective-permute-start | bytes 196616 | tf_op jit(solution)/shard_map/ppermute | solution.py:206
  5.3 5.7 %collective-permute-start = (f32[128,128]{1,0:T(8,128)S(1)}, f32[128,128]{1,0:T(8,128)S(1)}, u32[]{:S(2)}, u32[]{:S(2)}) collective-permute-start(f32[128,128]{1,0:T(8,128)S(1)} %pad_add_fusion.payload_ref), channel_id=1, source_target_pairs={{0,2},{1,3},{2,4},{3,5},{4,6},{5,7},{6,0},{7,1},{8,10},{9,11},{10,... | collective-permute-start | bytes 196616 | tf_op jit(solution)/shard_map/ppermute | solution.py:206
  6.2 0.8 %copy-start = (f32[64,64]{1,0:T(8,128)S(1)}, f32[64,64]{1,0:T(8,128)}, u32[]{:S(2)}) copy-start(f32[64,64]{1,0:T(8,128)} %factor_ref.3) | copy-start | bytes 49156
  6.9 0.8 %copy-start.4 = (f32[4,2048]{1,0:T(4,128)S(1)}, f32[4,2048]{1,0:T(4,128)}, u32[]{:S(2)}) copy-start(f32[4,2048]{1,0:T(4,128)} %row_panel_ref.1) | copy-start | bytes 98308
  11.0 1.6 %collective-permute-start.3 = (f32[4,128,128]{2,1,0:T(8,128)S(1)}, f32[4,128,128]{2,1,0:T(8,128)S(1)}, u32[]{:S(2)}, u32[]{:S(2)}) collective-permute-start(f32[4,128,128]{2,1,0:T(8,128)S(1)} %pad_maximum_fusion.near_ref), channel_id=1, source_target_pairs={{0,1},{1,0},{2,3},{3,2},{4,5},{5,4},{6,7},{7,6},{8,9},{9,8},{10,11... | collective-permute-start | bytes 786440 | tf_op jit(solution)/shard_map/ppermute | solution.py:230
  11.1 27.6 %slice-start.2 = ((s8[8388608]{0:T(1024)(128)(4,1)}), s8[4194304]{0:T(1024)(128)(4,1)S(1)}, s32[]{:S(2)}) async-start(s8[8388608]{0:T(1024)(128)(4,1)} %bitcast.6), calls=%async_computation.3 | async-start | bytes 8388608
  11.1 27.6 %copy-start.1 = (f32[64,64]{1,0:T(8,128)S(1)}, f32[64,64]{1,0:T(8,128)}, u32[]{:S(2)}) copy-start(f32[64,64]{1,0:T(8,128)} %factor_ref.3) | copy-start | bytes 49156
  11.1 27.5 %copy-start.2 = (f32[64,64]{1,0:T(8,128)S(1)}, f32[64,64]{1,0:T(8,128)}, u32[]{:S(2)}) copy-start(f32[64,64]{1,0:T(8,128)} %diag_grad_ref.1) | copy-start | bytes 49156
  11.1 27.5 %copy-start.3 = (f32[4,2048]{1,0:T(4,128)S(1)}, f32[4,2048]{1,0:T(4,128)}, u32[]{:S(2)}) copy-start(f32[4,2048]{1,0:T(4,128)} %row_grad_ref.1) | copy-start | bytes 98308
  12.6 26.1 %slice-start.3 = ((s8[8388608]{0:T(1024)(128)(4,1)}), s8[4194304]{0:T(1024)(128)(4,1)S(1)}, s32[]{:S(2)}) async-start(s8[8388608]{0:T(1024)(128)(4,1)} %bitcast.6), calls=%async_computation.4 | async-start | bytes 8388608

commit v6 on v5

--- a/solution.py
+++ b/solution.py
@@ -1,3 +1,5 @@
+import functools
+
 import jax
 import jax.numpy as jnp
 from jax import lax
@@ -41,7 +43,7 @@
 
 def prepare_kernel(
     payload_ref, factor_ref, row_panel_ref,
-    inverse_ref, copy_ref, rows_ref,
+    inverse_ref, solver_ref, copy_ref, rows_ref,
 ):
     copy_ref[...] = payload_ref[...]
     factor = factor_ref[...]
@@ -54,15 +56,18 @@
     value = eye
     for j in range(N - 1):
         value = value - below[:, j : j + 1] * value[j : j + 1, :]
-    inverse_ref[...] = value / diagonal_row
+    inverse = value / diagonal_row
+    inverse_ref[...] = inverse
+    high, middle, low = thirds(inverse.T)
+    solver_ref[...] = jnp.concatenate([high, high, high, middle, middle, low], axis=1)
     for j in range(PIECES):
         rows_ref[OWN * j : OWN * (j + 1), :] = row_panel_ref[:, 128 * j : 128 * (j + 1)]
 
 
-def solve_line(line_ref, inverse_ref, left_ref, first):
+def solve_line(line_ref, left_ref, first, solve):
     grads = jnp.concatenate([line_ref[k, :N, :] for k in range(4)], axis=1)
     panels = jnp.concatenate([line_ref[k, N:, :] for k in range(4)], axis=1)
-    solved = dot(inverse_ref[...], grads, (0, 0), HIGHEST)
+    solved = solve(grads)
     high, low = split(solved)
     both = jnp.concatenate([high, low], axis=0)
     panel_high, panel_low = split(panels)
@@ -89,6 +94,18 @@
 PACKED = 3 * HALF * HALF // 128
 
 
+def thirds(value):
+    high = value.astype(BF16)
+    rest = value - high.astype(F32)
+    middle = rest.astype(BF16)
+    return high, middle, (rest - middle.astype(F32)).astype(BF16)
+
+
+def solve_thirds(solver_ref, grads):
+    high, middle, low = thirds(grads)
+    return dot(solver_ref[...], jnp.concatenate([high, middle, low, high, middle, high], axis=0), (1, 0))
+
+
 def pack_lower(term):
     blocks = jnp.concatenate([term[:HALF, :HALF], term[HALF:, :HALF], term[HALF:, HALF:]], axis=1)
     rest = jnp.concatenate([blocks[PACKED:, HALF * i : HALF * (i + 1)] for i in range(3)], axis=0)
@@ -108,7 +125,7 @@
     own_hbm, left_ref, term_ref, part_ref,
     own, sem,
 ):
-    solved, both, term = solve_line(near_ref, inverse_ref, left_ref, 0)
+    solved, both, term = solve_line(near_ref, left_ref, 0, lambda g: dot(inverse_ref[...], g, (0, 0), HIGHEST))
     own[...] = solved[:, :LOCAL]
     copy = pltpu.make_async_copy(own, own_hbm, sem)
     copy.start()
@@ -120,13 +137,13 @@
 
 
 def far_kernel(
-    far_ref, inverse_ref, rows_ref, tile_ref, near_term_ref, near_part_ref, near_left_ref,
+    far_ref, solver_ref, rows_ref, tile_ref, near_term_ref, near_part_ref, near_left_ref,
     left_ref, send_ref,
 ):
     own_rows = rows_ref[...]
     for s in range(ROWS):
         send_ref[s, N : 2 * N, :] = own_rows
-    _, both, term = solve_line(far_ref, inverse_ref, left_ref, TILE_ROWS // 2)
+    _, both, term = solve_line(far_ref, left_ref, TILE_ROWS // 2, functools.partial(solve_thirds, solver_ref))
     term = term + near_term_ref[...]
     packed = pack_lower(term)
     for s in range(ROWS):
@@ -213,15 +230,16 @@
     opposite = across_chips(payload, 2)
     right = across_chips(payload, 1)
     left = across_chips(payload, 3)
-    inverse, payload, rows = pl.pallas_call(
+    inverse, solver, payload, rows = pl.pallas_call(
         prepare_kernel,
         out_shape=(
             jax.ShapeDtypeStruct((N, N), F32),
+            jax.ShapeDtypeStruct((N, 6 * N), BF16),
             jax.ShapeDtypeStruct((2 * N, LOCAL), F32),
             jax.ShapeDtypeStruct((N, 128), F32),
         ),
         in_specs=[vmem] * 3,
-        out_specs=(vmem,) * 3,
+        out_specs=(vmem,) * 4,
         compiler_params=pltpu.CompilerParams(vmem_limit_bytes=4 * MIB),
         cost_estimate=pl.CostEstimate(flops=4_000_000_000, bytes_accessed=0, transcendentals=0),
         name="prepare",
@@ -254,7 +272,7 @@
         input_output_aliases={6: 0},
         compiler_params=pltpu.CompilerParams(vmem_limit_bytes=16 * MIB),
         name="far",
-    )(far, inverse, rows, trailing, near_term, near_part, left_factor)
+    )(far, solver, rows, trailing, near_term, near_part, left_factor)
     recv = lax.all_to_all(send, "row", 0, 0, axis_index_groups=[ORDER])
     trailing_out, row_out, diag_out = pl.pallas_call(
         update_kernel,

time: 43 us -> 42.8 us (level)
  no operation moved by 1% of the time
where the time goes in v6:
time: 42.8 us; the launch traced here: 42.5 us
  blocking collectives  24.9 us (58%)
  Pallas kernels  7.11 us (17%)
  starting transfers between devices  4.67 us (11%)
  waiting for transfers between devices  2.56 us (6%)
  local copies, waits for them, and re-layouts  1.56 us (4%)
  other arithmetic  0.95 us (2%)
  between operations  0.77 us (2%)
    all_to_all x1, blocking collectives, per_device(): recv = lax.all_to_all(send, 'row', 0, 0, axis_index_groups=[ORDER])  24.9 us
    ppermute x3, starting transfers between devices, across_chips(): return lax.ppermute(value, 'col', pairs)  4.58 us
    pallas_call x1, Pallas kernels, per_device(): pl.pallas_call(update_kernel, out_shape=(jax.ShapeDtypeStruct((TILE_ROWS,...  3.91 us
    ppermute x3, waiting for transfers between devices, across_chips(): return lax.ppermute(value, 'col', pairs)  2.24 us
    unnamed x18, local copies, waits for them, and re-layouts  1.56 us
    pallas_call x1, Pallas kernels, per_device(): pl.pallas_call(near_kernel, out_shape=(jax.ShapeDtypeStruct((N, LOCAL), F...  1.12 us
    pallas_call x1, Pallas kernels, per_device(): pl.pallas_call(far_kernel, out_shape=(jax.ShapeDtypeStruct((TILE_ROWS, 4...  1.07 us
    pallas_call x1, Pallas kernels, per_device(): pl.pallas_call(prepare_kernel, out_shape=(jax.ShapeDtypeStruct((N, N), F3...  1.01 us
  transfers between devices with their start and end apart: 4, of which 3 were waited for; matrix products, arithmetic and copies ran while one was open for 0% of the time, Pallas kernels for 5%

profile of v6, /device:TPU:0, one launch (start us, length us, event | category | flops | bytes accessed | tf_op | source)
XLA Modules:
  0.0 42.5 jit_solution(17482235042742590736)
XLA Ops:
  0.6 0.0 slice-start
  0.6 0.9 %pad_add_fusion.payload_ref = f32[128,128]{1,0:T(8,128)S(1)} fusion(f32[64,128]{1,0:T(8,128)} %param.8, f32[64,128]{1,0:T(8,128)} %param.9), kind=kLoop, calls=%fused_computation.1 | loop fusion | flops 16384 | bytes 131072 | tf_op jit(solution)/shard_map/add | solution.py:229
  1.6 0.0 slice-start.1
  1.6 2.9 %collective-permute-start.2 = (f32[128,128]{1,0:T(8,128)S(1)}, f32[128,128]{1,0:T(8,128)S(1)}, u32[]{:S(2)}, u32[]{:S(2)}) collective-permute-start(f32[128,128]{1,0:T(8,128)S(1)} %pad_add_fusion.payload_ref), channel_id=1, source_target_pairs={{0,6},{1,7},{2,0},{3,1},{4,2},{5,3},{6,4},{7,5},{8,14},{9,15},{10,... | collective-permute-start | bytes 196616 | tf_op jit(solution)/shard_map/ppermute | solution.py:223
  4.5 0.8 %collective-permute-start.1 = (f32[128,128]{1,0:T(8,128)S(1)}, f32[128,128]{1,0:T(8,128)S(1)}, u32[]{:S(2)}, u32[]{:S(2)}) collective-permute-start(f32[128,128]{1,0:T(8,128)S(1)} %pad_add_fusion.payload_ref), channel_id=1, source_target_pairs={{0,4},{1,5},{2,6},{3,7},{4,0},{5,1},{6,2},{7,3},{8,12},{9,13},{10,... | collective-permute-start | bytes 196616 | tf_op jit(solution)/shard_map/ppermute | solution.py:223
  5.3 0.9 %collective-permute-start = (f32[128,128]{1,0:T(8,128)S(1)}, f32[128,128]{1,0:T(8,128)S(1)}, u32[]{:S(2)}, u32[]{:S(2)}) collective-permute-start(f32[128,128]{1,0:T(8,128)S(1)} %pad_add_fusion.payload_ref), channel_id=1, source_target_pairs={{0,2},{1,3},{2,4},{3,5},{4,6},{5,7},{6,0},{7,1},{8,10},{9,11},{10,... | collective-permute-start | bytes 196616 | tf_op jit(solution)/shard_map/ppermute | solution.py:223
  6.2 0.0 copy-start
  6.2 0.8 %copy-done = f32[64,64]{1,0:T(8,128)S(1)} copy-done((f32[64,64]{1,0:T(8,128)S(1)}, f32[64,64]{1,0:T(8,128)}, u32[]{:S(2)}) %copy-start) | copy-done | bytes 16408
  6.9 0.0 copy-start.4
  6.9 0.8 %copy-done.4 = f32[4,2048]{1,0:T(4,128)S(1)} copy-done((f32[4,2048]{1,0:T(4,128)S(1)}, f32[4,2048]{1,0:T(4,128)}, u32[]{:S(2)}) %copy-start.4) | copy-done | bytes 32792
  7.7 1.0 %prepare.1 = (f32[64,64]{1,0:T(8,128)S(1)}, bf16[64,384]{1,0:T(8,128)(2,1)S(1)}, f32[128,128]{1,0:T(8,128)S(1)}, f32[64,128]{1,0:T(8,128)S(1)}) custom-call(f32[128,128]{1,0:T(8,128)S(1)} %pad_add_fusion.payload_ref, f32[64,64]{1,0:T(8,128)S(1)} %copy-done, f32[4,2048]{1,0:T(4,128)S(1)} %copy-done.4), custom_call_target="tpu_custom_call" | custom-call | flops 4000000000 | tf_op jit(solution)/shard_map/prepare/pallas_call | solution.py:233
  8.7 0.0 collective-permute-done.2
  8.7 1.6 %collective-permute-done.1 = f32[128,128]{1,0:T(8,128)S(1)} collective-permute-done((f32[128,128]{1,0:T(8,128)S(1)}, f32[128,128]{1,0:T(8,128)S(1)}, u32[]{:S(2)}, u32[]{:S(2)}) %collective-permute-start.1) | collective-permute-done | bytes 65568 | tf_op jit(solution)/shard_map/ppermute | solution.py:223
  10.3 0.7 %collective-permute-done = f32[128,128]{1,0:T(8,128)S(1)} collective-permute-done((f32[128,128]{1,0:T(8,128)S(1)}, f32[128,128]{1,0:T(8,128)S(1)}, u32[]{:S(2)}, u32[]{:S(2)}) %collective-permute-start) | collective-permute-done | bytes 65568 | tf_op jit(solution)/shard_map/ppermute | solution.py:223
  11.0 0.1 collective-permute-start.3
  11.1 0.0 slice-done
  11.1 0.0 slice-done.1
  11.1 0.0 slice-start.2
  11.1 0.0 copy-start.1
  11.1 0.0 copy-start.2
  11.1 0.0 copy-start.3
  11.1 1.1 %near.1 = (f32[64,128]{1,0:T(8,128)}, bf16[1024,256]{1,0:T(8,128)(2,1)S(1)}, f32[64,64]{1,0:T(8,128)S(1)}, f32[64,2048]{1,0:T(8,128)S(1)}) custom-call(f32[4,128,128]{2,1,0:T(8,128)S(1)} %pad_maximum_fusion.near_ref, f32[64,64]{1,0:T(8,128)S(1)} %get-tuple-element.18.inverse_ref, f32[1024,2048]{1,0:T(8,128)S(1)} %bitcast.5), custom_call_target="tpu_custom_call" | custom-call | flops 1000000000 | tf_op jit(solution)/shard_map/near/pallas_call | solution.py:249
  12.3 0.3 collective-permute-done.3.far_ref
  12.6 0.0 slice-start.3
  12.6 1.1 %far.1 = (bf16[1024,256]{1,0:T(8,128)(2,1)S(1)}, f32[16,152,128]{2,1,0:T(8,128)S(1)}) custom-call(f32[4,128,128]{2,1,0:T(8,128)S(1)} %collective-permute-done.3.far_ref, bf16[64,384]{1,0:T(8,128)(2,1)S(1)} %get-tuple-element.20.solver_ref, f32[64,128]{1,0:T(8,128)S(1)} %get-tuple-element.21.rows_ref, ...), custom_call_target="tpu_custom_call", output_to_operand_aliasing={{0}: (6, {})} | custom-call | tf_op jit(solution)/shard_map/far/pallas_call | solution.py:264
  13.7 24.9 %all_to_all.5.recv_ref = f32[16,152,128]{2,1,0:T(8,128)S(1)} all-to-all(f32[16,152,128]{2,1,0:T(8,128)S(1)} %get-tuple-element.25), channel_id=1, replica_groups={{120,112,104,96,88,80,72,64,56,48,40,32,24,16,8,0},{121,113,105,97,89,8..., dimensions={0} | all-to-all | bytes 2490368 | tf_op jit(solution)/shard_map/all_to_all | solution.py:276
  38.6 0.0 slice-done.2
  38.6 0.0 copy-done.1
  38.6 0.0 copy-done.2
  38.6 0.0 copy-done.3
  38.6 0.0 slice-done.3
  38.6 3.9 %update.1 = (f32[1024,2048]{1,0:T(8,128)}, f32[4,2048]{1,0:T(4,128)}, f32[64,64]{1,0:T(8,128)}) custom-call(f32[16,152,128]{2,1,0:T(8,128)S(1)} %all_to_all.5.recv_ref, bf16[1024,256]{1,0:T(8,128)(2,1)S(1)} %get-tuple-element.26.left, f32[64,64]{1,0:T(8,128)S(1)} %get-tuple-element.18.inverse_ref, f32[64,64]{1,0:T(8,128)S(1)} %copy-done.1, ...), custom_call_target="tpu_custom_call" | custom-call | tf_op jit(solution)/shard_map/update/pallas_call | solution.py:277
  (3 shorter events, 0.0 us)
Async XLA Ops:
  0.6 10.4 %slice-start = ((s8[8388608]{0:T(1024)(128)(4,1)}), s8[4194304]{0:T(1024)(128)(4,1)S(1)}, s32[]{:S(2)}) async-start(s8[8388608]{0:T(1024)(128)(4,1)} %bitcast.4), calls=%async_computation.1 | async-start | bytes 8388608
  1.6 9.5 %slice-start.1 = ((s8[8388608]{0:T(1024)(128)(4,1)}), s8[4194304]{0:T(1024)(128)(4,1)S(1)}, s32[]{:S(2)}) async-start(s8[8388608]{0:T(1024)(128)(4,1)} %bitcast.4), calls=%async_computation.2 | async-start | bytes 8388608
  1.6 7.1 %collective-permute-start.2 = (f32[128,128]{1,0:T(8,128)S(1)}, f32[128,128]{1,0:T(8,128)S(1)}, u32[]{:S(2)}, u32[]{:S(2)}) collective-permute-start(f32[128,128]{1,0:T(8,128)S(1)} %pad_add_fusion.payload_ref), channel_id=1, source_target_pairs={{0,6},{1,7},{2,0},{3,1},{4,2},{5,3},{6,4},{7,5},{8,14},{9,15},{10,... | collective-permute-start | bytes 196616 | tf_op jit(solution)/shard_map/ppermute | solution.py:223
  4.5 5.8 %collective-permute-start.1 = (f32[128,128]{1,0:T(8,128)S(1)}, f32[128,128]{1,0:T(8,128)S(1)}, u32[]{:S(2)}, u32[]{:S(2)}) collective-permute-start(f32[128,128]{1,0:T(8,128)S(1)} %pad_add_fusion.payload_ref), channel_id=1, source_target_pairs={{0,4},{1,5},{2,6},{3,7},{4,0},{5,1},{6,2},{7,3},{8,12},{9,13},{10,... | collective-permute-start | bytes 196616 | tf_op jit(solution)/shard_map/ppermute | solution.py:223
  5.3 5.7 %collective-permute-start = (f32[128,128]{1,0:T(8,128)S(1)}, f32[128,128]{1,0:T(8,128)S(1)}, u32[]{:S(2)}, u32[]{:S(2)}) collective-permute-start(f32[128,128]{1,0:T(8,128)S(1)} %pad_add_fusion.payload_ref), channel_id=1, source_target_pairs={{0,2},{1,3},{2,4},{3,5},{4,6},{5,7},{6,0},{7,1},{8,10},{9,11},{10,... | collective-permute-start | bytes 196616 | tf_op jit(solution)/shard_map/ppermute | solution.py:223
  6.2 0.8 %copy-start = (f32[64,64]{1,0:T(8,128)S(1)}, f32[64,64]{1,0:T(8,128)}, u32[]{:S(2)}) copy-start(f32[64,64]{1,0:T(8,128)} %factor_ref.3) | copy-start | bytes 49156
  6.9 0.8 %copy-start.4 = (f32[4,2048]{1,0:T(4,128)S(1)}, f32[4,2048]{1,0:T(4,128)}, u32[]{:S(2)}) copy-start(f32[4,2048]{1,0:T(4,128)} %row_panel_ref.1) | copy-start | bytes 98308
  11.0 1.6 %collective-permute-start.3 = (f32[4,128,128]{2,1,0:T(8,128)S(1)}, f32[4,128,128]{2,1,0:T(8,128)S(1)}, u32[]{:S(2)}, u32[]{:S(2)}) collective-permute-start(f32[4,128,128]{2,1,0:T(8,128)S(1)} %pad_maximum_fusion.near_ref), channel_id=1, source_target_pairs={{0,1},{1,0},{2,3},{3,2},{4,5},{5,4},{6,7},{7,6},{8,9},{9,8},{10,11... | collective-permute-start | bytes 786440 | tf_op jit(solution)/shard_map/ppermute | solution.py:248
  11.1 27.5 %slice-start.2 = ((s8[8388608]{0:T(1024)(128)(4,1)}), s8[4194304]{0:T(1024)(128)(4,1)S(1)}, s32[]{:S(2)}) async-start(s8[8388608]{0:T(1024)(128)(4,1)} %bitcast.6), calls=%async_computation.3 | async-start | bytes 8388608
  11.1 27.5 %copy-start.1 = (f32[64,64]{1,0:T(8,128)S(1)}, f32[64,64]{1,0:T(8,128)}, u32[]{:S(2)}) copy-start(f32[64,64]{1,0:T(8,128)} %factor_ref.3) | copy-start | bytes 49156
  11.1 27.5 %copy-start.2 = (f32[64,64]{1,0:T(8,128)S(1)}, f32[64,64]{1,0:T(8,128)}, u32[]{:S(2)}) copy-start(f32[64,64]{1,0:T(8,128)} %diag_grad_ref.1) | copy-start | bytes 49156
  11.1 27.4 %copy-start.3 = (f32[4,2048]{1,0:T(4,128)S(1)}, f32[4,2048]{1,0:T(4,128)}, u32[]{:S(2)}) copy-start(f32[4,2048]{1,0:T(4,128)} %row_grad_ref.1) | copy-start | bytes 98308
  12.6 26.0 %slice-start.3 = ((s8[8388608]{0:T(1024)(128)(4,1)}), s8[4194304]{0:T(1024)(128)(4,1)S(1)}, s32[]{:S(2)}) async-start(s8[8388608]{0:T(1024)(128)(4,1)} %bitcast.6), calls=%async_computation.4 | async-start | bytes 8388608

commit v7 on v5

--- a/solution.py
+++ b/solution.py
@@ -13,8 +13,7 @@
 TILE_COLS = 2048
 OWN = N // ROWS
 PIECES = TILE_COLS // 128
-ORDER = [15, 14, 13, 12, 11, 10, 9, 8, 7, 6, 5, 4, 3, 2, 1, 0]
-SLOT = [15, 14, 13, 12, 11, 10, 9, 8, 7, 6, 5, 4, 3, 2, 1, 0]
+ORDER = tuple(range(ROWS - 1, -1, -1))
 HIGHEST = lax.Precision.HIGHEST
 F32 = jnp.float32
 BF16 = jnp.bfloat16
@@ -40,8 +39,8 @@
 
 
 def prepare_kernel(
-    payload_ref, factor_ref, row_panel_ref,
-    inverse_ref, copy_ref, rows_ref,
+    payload_ref, factor_ref,
+    inverse_ref, copy_ref,
 ):
     copy_ref[...] = payload_ref[...]
     factor = factor_ref[...]
@@ -55,8 +54,6 @@
     for j in range(N - 1):
         value = value - below[:, j : j + 1] * value[j : j + 1, :]
     inverse_ref[...] = value / diagonal_row
-    for j in range(PIECES):
-        rows_ref[OWN * j : OWN * (j + 1), :] = row_panel_ref[:, 128 * j : 128 * (j + 1)]
 
 
 def solve_line(line_ref, inverse_ref, left_ref, first):
@@ -120,40 +117,40 @@
 
 
 def far_kernel(
-    far_ref, inverse_ref, rows_ref, tile_ref, near_term_ref, near_part_ref, near_left_ref,
-    left_ref, send_ref,
-):
-    own_rows = rows_ref[...]
+    far_ref, inverse_ref, tile_ref, near_term_ref, near_part_ref, near_left_ref,
+    left_ref, send_hbm,
+    send, sems,
+):
+    _, both, term = solve_line(far_ref, inverse_ref, left_ref, TILE_ROWS // 2)
+    packed = pack_lower(term + near_term_ref[...])
     for s in range(ROWS):
-        send_ref[s, N : 2 * N, :] = own_rows
-    _, both, term = solve_line(far_ref, inverse_ref, left_ref, TILE_ROWS // 2)
-    term = term + near_term_ref[...]
-    packed = pack_lower(term)
-    for s in range(ROWS):
-        send_ref[s, 2 * N :, :] = packed
+        send[s, N:, :] = packed
+    copies = [pltpu.make_async_copy(send.at[:, N:], send_hbm.at[:, N:], sems.at[0])]
+    copies[0].start()
+    height = OWN * CHUNK // 128
     for i in range(TILE_COLS // CHUNK):
         cols = slice(i * CHUNK, (i + 1) * CHUNK)
         part = near_part_ref[:, cols] + line_product(both, tile_ref, cols, True)
         for s in range(ROWS):
             for jj in range(CHUNK // 128):
                 j = i * (CHUNK // 128) + jj
-                send_ref[SLOT[s], OWN * j : OWN * (j + 1), :] = part[OWN * s : OWN * (s + 1), 128 * jj : 128 * (jj + 1)]
+                send[ROWS - 1 - s, OWN * j : OWN * (j + 1), :] = part[OWN * s : OWN * (s + 1), 128 * jj : 128 * (jj + 1)]
+        slots = pl.ds(i * height, height)
+        copies.append(pltpu.make_async_copy(send.at[:, slots], send_hbm.at[:, slots], sems.at[i + 1]))
+        copies[-1].start()
+    for copy in copies:
+        copy.wait()
 
 
 def update_kernel(
-    recv_ref, left, inverse_ref, factor_ref, diag_grad_ref, row_grad_ref, grad_ref,
-    out_ref, row_out_hbm, diag_out_hbm,
-    result, full, right, small, row_out, diag_out, out_sems, small_sems,
+    rows_ref, left, grad_ref,
+    out_ref, right,
+    result, out_sems,
 ):
     stores = []
-    edges = [0, 256, 512, 768, 1024, 1280, 1536, 1792, 2048]
-
-    def step(i):
-        cols = slice(edges[i], edges[i + 1])
-        for s in range(ROWS):
-            for j in range(edges[i] // 128, edges[i + 1] // 128):
-                full[OWN * s : OWN * (s + 1), 128 * j : 128 * (j + 1)] = recv_ref[SLOT[s], N + OWN * j : N + OWN * (j + 1), :]
-        high, low = split(full[:, cols])
+    for i in range(TILE_COLS // CHUNK):
+        cols = slice(i * CHUNK, (i + 1) * CHUNK)
+        high, low = split(jnp.concatenate([rows_ref[ROWS - 1 - s, :, cols] for s in range(ROWS)], axis=0))
         right[:, cols] = jnp.concatenate([high, high, low, low], axis=0)
         product = dot(left[...], right[:, cols], (1, 0))
         for slot in range(COLS):
@@ -161,15 +158,19 @@
             result[part, cols] = grad_ref[part, cols] - product[slot * LOCAL : (slot + 1) * LOCAL]
         stores.append(pltpu.make_async_copy(result.at[:, cols], out_ref.at[:, cols], out_sems.at[i]))
         stores[-1].start()
-
-    count = len(edges) - 1
-    for i in range(4):
-        step(i)
-
-    packed = recv_ref[0, 2 * N :, :]
+    for copy in stores:
+        copy.wait()
+
+
+def final_kernel(
+    recv_ref, right, inverse_ref, factor_ref, diag_grad_ref, row_grad_ref,
+    row_out_hbm, diag_out_hbm,
+    small, row_out, diag_out, sems,
+):
+    packed = recv_ref[0, N:, :]
     reduced = recv_ref[0, :N, :]
     for s in range(1, ROWS):
-        packed = packed + recv_ref[s, 2 * N :, :]
+        packed = packed + recv_ref[s, N:, :]
         reduced = reduced + recv_ref[s, :N, :]
     total = unpack_lower(packed)
     inverse, factor = inverse_ref[...], factor_ref[...]
@@ -182,23 +183,20 @@
     spart = dot(dot(inverse, phi, (0, 0), HIGHEST), inverse, (1, 0), HIGHEST)
     both = spart + spart.T
     diag_out[...] = 0.5 * both
-    stores.append(pltpu.make_async_copy(diag_out, diag_out_hbm, small_sems.at[0]))
-    stores[-1].start()
+    first = pltpu.make_async_copy(diag_out, diag_out_hbm, sems.at[0])
+    first.start()
     small[...] = both
     own_both = small[pl.ds(lax.axis_index("row") * OWN, OWN), :]
     both_high, both_low = split(own_both)
     wide = jnp.concatenate([both_high, both_low, both_high, both_low], axis=1)
-
-    for i in range(4, count):
-        step(i)
     second = dot(wide, right[...], (1, 0))
     for j in range(PIECES):
         cols = slice(128 * j, 128 * (j + 1))
         row_out[:, cols] = row_grad_ref[:, cols] - reduced[OWN * j : OWN * (j + 1), :] - second[:, cols]
-    stores.append(pltpu.make_async_copy(row_out, row_out_hbm, small_sems.at[1]))
-    stores[-1].start()
-    for copy in stores:
-        copy.wait()
+    last = pltpu.make_async_copy(row_out, row_out_hbm, sems.at[1])
+    last.start()
+    first.wait()
+    last.wait()
 
 
 def across_chips(value, k):
@@ -213,19 +211,19 @@
     opposite = across_chips(payload, 2)
     right = across_chips(payload, 1)
     left = across_chips(payload, 3)
-    inverse, payload, rows = pl.pallas_call(
+    rows = lax.all_to_all(jnp.broadcast_to(row_panel[None], (ROWS, OWN, TILE_COLS)), "row", 0, 0, axis_index_groups=[ORDER])
+    inverse, payload = pl.pallas_call(
         prepare_kernel,
         out_shape=(
             jax.ShapeDtypeStruct((N, N), F32),
             jax.ShapeDtypeStruct((2 * N, LOCAL), F32),
-            jax.ShapeDtypeStruct((N, 128), F32),
-        ),
-        in_specs=[vmem] * 3,
-        out_specs=(vmem,) * 3,
+        ),
+        in_specs=[vmem] * 2,
+        out_specs=(vmem,) * 2,
         compiler_params=pltpu.CompilerParams(vmem_limit_bytes=4 * MIB),
-        cost_estimate=pl.CostEstimate(flops=4_000_000_000, bytes_accessed=0, transcendentals=0),
+        cost_estimate=pl.CostEstimate(flops=20000000000, bytes_accessed=0, transcendentals=0),
         name="prepare",
-    )(payload, diag_factor, row_panel)
+    )(payload, diag_factor)
     near = jnp.stack([payload, right, opposite, left])
     far = lax.ppermute(near, "col", [(i, i ^ 1) for i in range(COLS)])
     panel_out, left_factor, near_term, near_part = pl.pallas_call(
@@ -240,44 +238,54 @@
         out_specs=(anywhere,) + (vmem,) * 3,
         scratch_shapes=[pltpu.VMEM((N, LOCAL), F32), pltpu.SemaphoreType.DMA],
         compiler_params=pltpu.CompilerParams(vmem_limit_bytes=16 * MIB),
-        cost_estimate=pl.CostEstimate(flops=1_000_000_000, bytes_accessed=0, transcendentals=0),
+        cost_estimate=pl.CostEstimate(flops=4000000000, bytes_accessed=0, transcendentals=0),
         name="near",
     )(near, inverse, trailing)
     left_factor, send = pl.pallas_call(
         far_kernel,
         out_shape=(
             jax.ShapeDtypeStruct((TILE_ROWS, 4 * N), BF16),
-            jax.ShapeDtypeStruct((ROWS, 2 * N + PACKED, 128), F32),
-        ),
-        in_specs=[vmem] * 6 + [anywhere],
-        out_specs=(vmem,) * 2,
-        input_output_aliases={6: 0},
-        compiler_params=pltpu.CompilerParams(vmem_limit_bytes=16 * MIB),
+            jax.ShapeDtypeStruct((ROWS, N + PACKED, 128), F32),
+        ),
+        in_specs=[vmem] * 5 + [anywhere],
+        out_specs=(vmem, anywhere),
+        scratch_shapes=[pltpu.VMEM((ROWS, N + PACKED, 128), F32), pltpu.SemaphoreType.DMA((9,))],
+        input_output_aliases={5: 0},
+        compiler_params=pltpu.CompilerParams(vmem_limit_bytes=20 * MIB),
+        cost_estimate=pl.CostEstimate(flops=4_000_000_000, bytes_accessed=0, transcendentals=0),
         name="far",
-    )(far, inverse, rows, trailing, near_term, near_part, left_factor)
+    )(far, inverse, trailing, near_term, near_part, left_factor)
     recv = lax.all_to_all(send, "row", 0, 0, axis_index_groups=[ORDER])
-    trailing_out, row_out, diag_out = pl.pallas_call(
+    trailing_out, right_factor = pl.pallas_call(
         update_kernel,
         out_shape=(
             jax.ShapeDtypeStruct((TILE_ROWS, TILE_COLS), F32),
+            jax.ShapeDtypeStruct((4 * N, TILE_COLS), BF16),
+        ),
+        in_specs=[vmem] * 3,
+        out_specs=(anywhere, vmem),
+        scratch_shapes=[pltpu.VMEM((TILE_ROWS, TILE_COLS), F32), pltpu.SemaphoreType.DMA((8,))],
+        compiler_params=pltpu.CompilerParams(vmem_limit_bytes=32 * MIB),
+        cost_estimate=pl.CostEstimate(flops=4_000_000_000, bytes_accessed=0, transcendentals=0),
+        name="update",
+    )(rows, left_factor, trailing_grad)
+    row_out, diag_out = pl.pallas_call(
+        final_kernel,
+        out_shape=(
             jax.ShapeDtypeStruct((OWN, TILE_COLS), F32),
             jax.ShapeDtypeStruct((N, N), F32),
         ),
-        in_specs=[vmem] * 7,
-        out_specs=(anywhere,) * 3,
+        in_specs=[vmem] * 6,
+        out_specs=(anywhere,) * 2,
         scratch_shapes=[
-            pltpu.VMEM((TILE_ROWS, TILE_COLS), F32),
-            pltpu.VMEM((N, TILE_COLS), F32),
-            pltpu.VMEM((4 * N, TILE_COLS), BF16),
             pltpu.VMEM((N, N), F32),
             pltpu.VMEM((OWN, TILE_COLS), F32),
             pltpu.VMEM((N, N), F32),
-            pltpu.SemaphoreType.DMA((8,)),
             pltpu.SemaphoreType.DMA((2,)),
         ],
-        compiler_params=pltpu.CompilerParams(vmem_limit_bytes=32 * MIB),
-        name="update",
-    )(recv, left_factor, inverse, diag_factor, diag_grad, row_grad, trailing_grad)
+        compiler_params=pltpu.CompilerParams(vmem_limit_bytes=8 * MIB),
+        name="final",
+    )(recv, right_factor, inverse, diag_factor, diag_grad, row_grad)
     return (panel_out, trailing_out, row_out, diag_out)
 
 

time: 43 us -> 43 us (level)
  the two profiles are of different devices: /device:TPU:0 before, /device:TPU:2 now
where the time goes in v7:
time: 43 us; the launch traced here: 42.4 us
  starting transfers between devices  22 us (51%)
  Pallas kernels  9.44 us (22%)
  local copies, waits for them, and re-layouts  8.18 us (19%)
  waiting for transfers between devices  1.15 us (3%)
  other arithmetic  0.8 us (2%)
  between operations  0.76 us (2%)
    all_to_all x1, starting transfers between devices, per_device(): lax.all_to_all(jnp.broadcast_to(row_panel[None], (ROWS, OWN, TILE_COLS)),...  9.95 us
    all_to_all x1, starting transfers between devices, per_device(): recv = lax.all_to_all(send, 'row', 0, 0, axis_index_groups=[ORDER])  7.24 us
    unnamed x12, local copies, waits for them, and re-layouts  6.53 us
    ppermute x3, starting transfers between devices, across_chips(): return lax.ppermute(value, 'col', pairs)  4.76 us
    pallas_call x1, Pallas kernels, per_device(): pl.pallas_call(update_kernel, out_shape=(jax.ShapeDtypeStruct((TILE_ROWS,...  3.85 us
    pallas_call x1, Pallas kernels, per_device(): pl.pallas_call(far_kernel, out_shape=(jax.ShapeDtypeStruct((TILE_ROWS, 4...  1.92 us
    pallas_call x1, Pallas kernels, per_device(): pl.pallas_call(final_kernel, out_shape=(jax.ShapeDtypeStruct((OWN, TILE_C...  1.7 us
    broadcast_in_dim x1, local copies, waits for them, and re-layouts, per_device(): jnp.broadcast_to(row_panel[None], (ROWS, OWN, TILE_COLS))  1.65 us
  transfers between devices with their start and end apart: 6, of which 1 were waited for; matrix products, arithmetic and copies ran while one was open for 4% of the time, Pallas kernels for 18%

profile of v7, /device:TPU:2, one launch (start us, length us, event | category | flops | bytes accessed | tf_op | source)
XLA Modules:
  0.0 42.4 jit_solution(13188047654253085604)
XLA Ops:
  0.6 0.8 %pad_add_fusion.payload_ref = f32[128,128]{1,0:T(8,128)S(1)} fusion(f32[64,128]{1,0:T(8,128)} %param.8, f32[64,128]{1,0:T(8,128)} %param.9), kind=kLoop, calls=%fused_computation.1 | loop fusion | flops 16384 | bytes 131072 | tf_op jit(solution)/shard_map/add | solution.py:210
  1.4 0.5 %collective-permute-start.2 = (f32[128,128]{1,0:T(8,128)S(1)}, f32[128,128]{1,0:T(8,128)S(1)}, u32[]{:S(2)}, u32[]{:S(2)}) collective-permute-start(f32[128,128]{1,0:T(8,128)S(1)} %pad_add_fusion.payload_ref), channel_id=1, source_target_pairs={{0,6},{1,7},{2,0},{3,1},{4,2},{5,3},{6,4},{7,5},{8,14},{9,15},{10,... | collective-permute-start | bytes 196616 | tf_op jit(solution)/shard_map/ppermute | solution.py:204
  1.9 2.5 %collective-permute-start.1 = (f32[128,128]{1,0:T(8,128)S(1)}, f32[128,128]{1,0:T(8,128)S(1)}, u32[]{:S(2)}, u32[]{:S(2)}) collective-permute-start(f32[128,128]{1,0:T(8,128)S(1)} %pad_add_fusion.payload_ref), channel_id=1, source_target_pairs={{0,4},{1,5},{2,6},{3,7},{4,0},{5,1},{6,2},{7,3},{8,12},{9,13},{10,... | collective-permute-start | bytes 196616 | tf_op jit(solution)/shard_map/ppermute | solution.py:204
  4.4 1.8 %collective-permute-start = (f32[128,128]{1,0:T(8,128)S(1)}, f32[128,128]{1,0:T(8,128)S(1)}, u32[]{:S(2)}, u32[]{:S(2)}) collective-permute-start(f32[128,128]{1,0:T(8,128)S(1)} %pad_add_fusion.payload_ref), channel_id=1, source_target_pairs={{0,2},{1,3},{2,4},{3,5},{4,6},{5,7},{6,0},{7,1},{8,10},{9,11},{10,... | collective-permute-start | bytes 196616 | tf_op jit(solution)/shard_map/ppermute | solution.py:204
  6.2 1.7 %broadcast_in_dim.2 = f32[16,4,2048]{2,1,0:T(4,128)} broadcast(f32[4,2048]{1,0:T(4,128)} %param.12), dimensions={1,2} | broadcast | bytes 557056 | tf_op jit(solution)/shard_map/broadcast_in_dim | solution.py:214
  7.8 9.9 %all-to-all-start = ((f32[16,4,2048]{2,1,0:T(4,128)}), f32[16,4,2048]{2,1,0:T(4,128)S(1)}, u32[]{:S(2)}, u32[]{:S(2)}) async-start(f32[16,4,2048]{2,1,0:T(4,128)} %broadcast_in_dim.2), calls=%async_computation | async-start | bytes 1048576 | tf_op jit(solution)/shard_map/all_to_all | solution.py:214
  17.8 0.0 copy-start
  17.8 0.8 %copy-done = f32[64,64]{1,0:T(8,128)S(1)} copy-done((f32[64,64]{1,0:T(8,128)S(1)}, f32[64,64]{1,0:T(8,128)}, u32[]{:S(2)}) %copy-start) | copy-done | bytes 16408
  18.5 0.0 copy-start.4
  18.5 0.8 %prepare.1 = (f32[64,64]{1,0:T(8,128)S(1)}, f32[128,128]{1,0:T(8,128)S(1)}) custom-call(f32[128,128]{1,0:T(8,128)S(1)} %pad_add_fusion.payload_ref, f32[64,64]{1,0:T(8,128)S(1)} %copy-done), custom_call_target="tpu_custom_call" | custom-call | flops 20000000000 | tf_op jit(solution)/shard_map/prepare/pallas_call | solution.py:215
  19.4 0.0 collective-permute-done.2
  19.4 0.0 collective-permute-done.1
  19.4 0.0 collective-permute-done
  19.4 0.1 collective-permute-start.3
  19.5 2.4 %copy-done.4 = f32[1024,2048]{1,0:T(8,128)S(1)} copy-done((f32[1024,2048]{1,0:T(8,128)S(1)}, f32[1024,2048]{1,0:T(8,128)}, u32[]{:S(2)}) %copy-start.4) | copy-done | bytes 8388632
  21.9 1.1 %near.1 = (f32[64,128]{1,0:T(8,128)}, bf16[1024,256]{1,0:T(8,128)(2,1)S(1)}, f32[64,64]{1,0:T(8,128)S(1)}, f32[64,2048]{1,0:T(8,128)S(1)}) custom-call(f32[4,128,128]{2,1,0:T(8,128)S(1)} %pad_maximum_fusion.near_ref, f32[64,64]{1,0:T(8,128)S(1)} %get-tuple-element.17.inverse_ref, f32[1024,2048]{1,0:T(8,128)S(1)} %copy-done.4), custom_call_target="tpu_custom_call" | custom-call | flops 4000000000 | tf_op jit(solution)/shard_map/near/pallas_call | solution.py:229
  23.0 0.0 collective-permute-done.3.far_ref
  23.1 1.9 %far.1 = (bf16[1024,256]{1,0:T(8,128)(2,1)S(1)}, f32[16,88,128]{2,1,0:T(8,128)}) custom-call(f32[4,128,128]{2,1,0:T(8,128)S(1)} %collective-permute-done.3.far_ref, f32[64,64]{1,0:T(8,128)S(1)} %get-tuple-element.17.inverse_ref, f32[1024,2048]{1,0:T(8,128)S(1)} %copy-done.4, ...), custom_call_target="tpu_custom_call", output_to_operand_aliasing={{0}: (5, {})} | custom-call | flops 4000000000 | tf_op jit(solution)/shard_map/far/pallas_call | solution.py:244
  25.0 0.0 copy-start.1
  25.0 0.0 copy-start.2
  25.0 0.0 copy-start.3
  25.0 0.0 all-to-all-done.rows_ref
  25.0 7.2 %all-to-all-start.1 = ((f32[16,88,128]{2,1,0:T(8,128)}), f32[16,88,128]{2,1,0:T(8,128)S(1)}, u32[]{:S(2)}, u32[]{:S(2)}) async-start(f32[16,88,128]{2,1,0:T(8,128)} %get-tuple-element.24), calls=%async_computation.1 | async-start | bytes 1441792 | tf_op jit(solution)/shard_map/all_to_all | solution.py:258
  32.3 0.0 copy-start.5
  32.3 3.4 %copy-done.5 = f32[1024,2048]{1,0:T(8,128)S(1)} copy-done((f32[1024,2048]{1,0:T(8,128)S(1)}, f32[1024,2048]{1,0:T(8,128)}, u32[]{:S(2)}) %copy-start.5) | copy-done | bytes 8388632
  35.7 3.9 %update.1 = (f32[1024,2048]{1,0:T(8,128)}, bf16[256,2048]{1,0:T(8,128)(2,1)S(1)}) custom-call(f32[16,4,2048]{2,1,0:T(4,128)S(1)} %all-to-all-done.rows_ref, bf16[1024,256]{1,0:T(8,128)(2,1)S(1)} %get-tuple-element.22.left, f32[1024,2048]{1,0:T(8,128)S(1)} %copy-done.5), custom_call_target="tpu_custom_call" | custom-call | flops 4000000000 | tf_op jit(solution)/shard_map/update/pallas_call | solution.py:259
  39.5 1.1 %all-to-all-done.1.recv_ref = f32[16,88,128]{2,1,0:T(8,128)S(1)} async-done(((f32[16,88,128]{2,1,0:T(8,128)}), f32[16,88,128]{2,1,0:T(8,128)S(1)}, u32[]{:S(2)}, u32[]{:S(2)}) %all-to-all-start.1) | async-done | bytes 720928 | tf_op jit(solution)/shard_map/all_to_all | solution.py:258
  40.6 0.0 copy-done.1
  40.6 0.0 copy-done.2
  40.6 0.0 copy-done.3
  40.7 1.7 %final.1 = (f32[4,2048]{1,0:T(4,128)}, f32[64,64]{1,0:T(8,128)}) custom-call(f32[16,88,128]{2,1,0:T(8,128)S(1)} %all-to-all-done.1.recv_ref, bf16[256,2048]{1,0:T(8,128)(2,1)S(1)} %get-tuple-element.25.right, f32[64,64]{1,0:T(8,128)S(1)} %get-tuple-element.17.inverse_ref, f32[64,64]{1,0:T(8,128)S(1)} %copy-done.1, f32[64,64]{1,0:T(8,128)S(1)} %copy-done.2, ...), custom_call_target="tpu_custom_call" | custom-call | tf_op jit(solution)/shard_map/final/pallas_call | solution.py:272
  (1 shorter events, 0.0 us)
Async XLA Ops:
  1.4 18.0 %collective-permute-start.2 = (f32[128,128]{1,0:T(8,128)S(1)}, f32[128,128]{1,0:T(8,128)S(1)}, u32[]{:S(2)}, u32[]{:S(2)}) collective-permute-start(f32[128,128]{1,0:T(8,128)S(1)} %pad_add_fusion.payload_ref), channel_id=1, source_target_pairs={{0,6},{1,7},{2,0},{3,1},{4,2},{5,3},{6,4},{7,5},{8,14},{9,15},{10,... | collective-permute-start | bytes 196616 | tf_op jit(solution)/shard_map/ppermute | solution.py:204
  1.9 17.5 %collective-permute-start.1 = (f32[128,128]{1,0:T(8,128)S(1)}, f32[128,128]{1,0:T(8,128)S(1)}, u32[]{:S(2)}, u32[]{:S(2)}) collective-permute-start(f32[128,128]{1,0:T(8,128)S(1)} %pad_add_fusion.payload_ref), channel_id=1, source_target_pairs={{0,4},{1,5},{2,6},{3,7},{4,0},{5,1},{6,2},{7,3},{8,12},{9,13},{10,... | collective-permute-start | bytes 196616 | tf_op jit(solution)/shard_map/ppermute | solution.py:204
  4.4 15.0 %collective-permute-start = (f32[128,128]{1,0:T(8,128)S(1)}, f32[128,128]{1,0:T(8,128)S(1)}, u32[]{:S(2)}, u32[]{:S(2)}) collective-permute-start(f32[128,128]{1,0:T(8,128)S(1)} %pad_add_fusion.payload_ref), channel_id=1, source_target_pairs={{0,2},{1,3},{2,4},{3,5},{4,6},{5,7},{6,0},{7,1},{8,10},{9,11},{10,... | collective-permute-start | bytes 196616 | tf_op jit(solution)/shard_map/ppermute | solution.py:204
  7.8 17.2 %all-to-all-start = ((f32[16,4,2048]{2,1,0:T(4,128)}), f32[16,4,2048]{2,1,0:T(4,128)S(1)}, u32[]{:S(2)}, u32[]{:S(2)}) async-start(f32[16,4,2048]{2,1,0:T(4,128)} %broadcast_in_dim.2), calls=%async_computation | async-start | bytes 1048576 | tf_op jit(solution)/shard_map/all_to_all | solution.py:214
  17.8 0.8 %copy-start = (f32[64,64]{1,0:T(8,128)S(1)}, f32[64,64]{1,0:T(8,128)}, u32[]{:S(2)}) copy-start(f32[64,64]{1,0:T(8,128)} %factor_ref.3) | copy-start | bytes 49156
  18.5 3.4 %copy-start.4 = (f32[1024,2048]{1,0:T(8,128)S(1)}, f32[1024,2048]{1,0:T(8,128)}, u32[]{:S(2)}) copy-start(f32[1024,2048]{1,0:T(8,128)} %tile_ref.3) | copy-start | bytes 25165828
  19.4 3.6 %collective-permute-start.3 = (f32[4,128,128]{2,1,0:T(8,128)S(1)}, f32[4,128,128]{2,1,0:T(8,128)S(1)}, u32[]{:S(2)}, u32[]{:S(2)}) collective-permute-start(f32[4,128,128]{2,1,0:T(8,128)S(1)} %pad_maximum_fusion.near_ref), channel_id=1, source_target_pairs={{0,1},{1,0},{2,3},{3,2},{4,5},{5,4},{6,7},{7,6},{8,9},{9,8},{10,11... | collective-permute-start | bytes 786440 | tf_op jit(solution)/shard_map/ppermute | solution.py:228
  25.0 15.7 %copy-start.1 = (f32[64,64]{1,0:T(8,128)S(1)}, f32[64,64]{1,0:T(8,128)}, u32[]{:S(2)}) copy-start(f32[64,64]{1,0:T(8,128)} %factor_ref.3) | copy-start | bytes 49156
  25.0 15.7 %copy-start.2 = (f32[64,64]{1,0:T(8,128)S(1)}, f32[64,64]{1,0:T(8,128)}, u32[]{:S(2)}) copy-start(f32[64,64]{1,0:T(8,128)} %diag_grad_ref.1) | copy-start | bytes 49156
  25.0 15.6 %copy-start.3 = (f32[4,2048]{1,0:T(4,128)S(1)}, f32[4,2048]{1,0:T(4,128)}, u32[]{:S(2)}) copy-start(f32[4,2048]{1,0:T(4,128)} %row_grad_ref.1) | copy-start | bytes 98308
  25.0 15.6 %all-to-all-start.1 = ((f32[16,88,128]{2,1,0:T(8,128)}), f32[16,88,128]{2,1,0:T(8,128)S(1)}, u32[]{:S(2)}, u32[]{:S(2)}) async-start(f32[16,88,128]{2,1,0:T(8,128)} %get-tuple-element.24), calls=%async_computation.1 | async-start | bytes 1441792 | tf_op jit(solution)/shard_map/all_to_all | solution.py:258
  32.3 3.4 %copy-start.5 = (f32[1024,2048]{1,0:T(8,128)S(1)}, f32[1024,2048]{1,0:T(8,128)}, u32[]{:S(2)}) copy-start(f32[1024,2048]{1,0:T(8,128)} %grad_ref.1) | copy-start | bytes 25165828
